TPU v7x, 128 devices: a whole 4x4x4 slice. The times are simulated.
128 devices in a mesh: fsdp: 32 (over z, y, x_hi), ctx: 2 (over core), tp: 2 (over x_lo).
Axes of the slice: x: 4 (x_hi: 2, x_lo: 2; x = x_hi * 2 + x_lo), y: 4, z: 4, core: 2. Of those that a mesh axis runs over, the one named last changes fastest.
Arguments:
- tokens: bfloat16 [8192, 512], P(('fsdp', 'ctx')), may hold values from -16 to 16
- positions: int32 [8192], P(('fsdp', 'ctx')), may hold values from 0 to 2047, as said below
- cotangent: bfloat16 [8192, 512], P(('fsdp', 'ctx')), may hold values from -16 to 16
- ln1_gain: bfloat16 [1, 512], P(None, 'fsdp'), may hold values from 0.099609375 to 1.8984375
- ln1_bias: bfloat16 [1, 512], P(None, 'fsdp'), may hold values from -2 to 2
- ln2_gain: bfloat16 [1, 512], P(None, 'fsdp'), may hold values from 0.099609375 to 1.8984375
- ln2_bias: bfloat16 [1, 512], P(None, 'fsdp'), may hold values from -2 to 2
- qkv_weight: bfloat16 [1, 3, 512, 512], P(None, None, 'fsdp', 'tp'), may hold values from -0.25 to 0.25
- qkv_bias: bfloat16 [1, 3, 8, 64], P(None, None, 'tp', 'fsdp'), may hold values from -2 to 2
- out_weight: bfloat16 [1, 512, 512], P(None, 'tp', 'fsdp'), may hold values from -0.75 to 0.75
- out_bias: bfloat16 [1, 512], P(None, 'fsdp'), may hold values from -2 to 2
- up_weight: bfloat16 [1, 512, 2048], P(None, 'fsdp', 'tp'), may hold values from -0.25 to 0.25
- up_bias: bfloat16 [1, 32, 64], P(None, 'tp', 'fsdp'), may hold values from -2 to 2
- down_weight: bfloat16 [1, 2048, 512], P(None, 'tp', 'fsdp'), may hold values from -0.125 to 0.125
- down_bias: bfloat16 [1, 512], P(None, 'fsdp'), may hold values from -2 to 2
Outputs:
- output: bfloat16 [8192, 512], P(('fsdp', 'ctx'))
- grad_input: float32 [8192, 512], P(('fsdp', 'ctx'))
- grad_ln1_gain: float32 [1, 512], P(None, 'fsdp')
- grad_ln1_bias: float32 [1, 512], P(None, 'fsdp')
- grad_ln2_gain: float32 [1, 512], P(None, 'fsdp')
- grad_ln2_bias: float32 [1, 512], P(None, 'fsdp')
- grad_qkv_weight: float32 [1, 3, 512, 512], P(None, None, 'fsdp', 'tp')
- grad_qkv_bias: float32 [1, 3, 8, 64], P(None, None, 'tp', 'fsdp')
- grad_out_weight: float32 [1, 512, 512], P(None, 'tp', 'fsdp')
- grad_out_bias: float32 [1, 512], P(None, 'fsdp')
- grad_up_weight: float32 [1, 512, 2048], P(None, 'fsdp', 'tp')
- grad_up_bias: float32 [1, 32, 64], P(None, 'tp', 'fsdp')
- grad_down_weight: float32 [1, 2048, 512], P(None, 'tp', 'fsdp')
- grad_down_bias: float32 [1, 512], P(None, 'fsdp')
Inputs may be any that keep to these rules, and one draw needn't show every extreme that they name: Each sequence of 256 tokens begins inside a document whose positions count up by one from some start, and from some token at or after 3 * 64 may begin a second document whose positions count up from 0.
All inputs are finite; a program needn't handle non-finite values.
Results may differ from a plain program's by a relative error of at most 0.025.
Values may be sent and summed in bfloat16 or wider, within the bound.
A program may use at most 64 MiB of HBM per device.

v0:
```python
import math

import jax
import jax.numpy as jnp
from jax import lax
from jax.sharding import PartitionSpec as P

HD = 64
ROT = 16


EPS = 1e-05
BASE = 10000.0
MASKED = -1e30
INV_ROOT_TWO = 1.0 / math.sqrt(2.0)
INV_ROOT_TWO_PI = 1.0 / math.sqrt(2.0 * math.pi)


def layer_norm(inputs, scale_vec, shift_vec):
    row_mean = jnp.mean(inputs, axis=-1, keepdims=True)
    centered = inputs - row_mean
    moment = jnp.mean(centered * centered, axis=-1, keepdims=True)
    return centered * lax.rsqrt(moment + EPS) * scale_vec + shift_vec


def turn_tables(places):
    half_rot = ROT // 2
    freq_index = jnp.arange(half_rot, dtype=jnp.float32)
    inverse = BASE ** (-2.0 * freq_index / ROT)
    angles = places.astype(jnp.float32)[..., None] * inverse
    return (jnp.cos(angles), jnp.sin(angles))


def rotate(inputs, cos_table, sin_table):
    half_rot = ROT // 2
    cos_heads = cos_table[..., None, :]
    sin_heads = sin_table[..., None, :]
    low_part = inputs[..., :half_rot]
    high_part = inputs[..., half_rot:ROT]
    return jnp.concatenate(
        [
            low_part * cos_heads - high_part * sin_heads,
            high_part * cos_heads + low_part * sin_heads,
            inputs[..., ROT:],
        ],
        axis=-1,
    )


def score_block(query_heads, key_heads, visible):
    score_scale = 1.0 / math.sqrt(HD)
    raw_scores = (
        jnp.einsum("shd,thd->hst", query_heads, key_heads, preferred_element_type=jnp.float32)
        * score_scale
    )
    return jnp.where(visible[None], raw_scores, MASKED)


def gather_layer(parts):
    return (
        lax.all_gather(parts[0], "fsdp", axis=0, tiled=True),
        lax.all_gather(parts[1], "fsdp", axis=0, tiled=True),
        lax.all_gather(parts[2], "fsdp", axis=0, tiled=True),
        lax.all_gather(parts[3], "fsdp", axis=0, tiled=True),
        lax.all_gather(parts[4], "fsdp", axis=1, tiled=True),
        lax.all_gather(parts[5], "fsdp", axis=2, tiled=True),
        lax.all_gather(parts[6], "fsdp", axis=1, tiled=True),
        lax.all_gather(parts[7], "fsdp", axis=0, tiled=True),
        lax.all_gather(parts[8], "fsdp", axis=0, tiled=True),
        lax.all_gather(parts[9], "fsdp", axis=1, tiled=True),
        lax.all_gather(parts[10], "fsdp", axis=1, tiled=True),
        lax.all_gather(parts[11], "fsdp", axis=0, tiled=True),
    )


def gather_again(parts):
    return (
        lax.all_gather(parts[0], "fsdp", axis=0, tiled=True),
        lax.all_gather(parts[1], "fsdp", axis=0, tiled=True),
        lax.all_gather(parts[2], "fsdp", axis=0, tiled=True),
        lax.all_gather(parts[3], "fsdp", axis=0, tiled=True),
        lax.all_gather(parts[4], "fsdp", axis=1, tiled=True),
        lax.all_gather(parts[5], "fsdp", axis=2, tiled=True),
        lax.all_gather(parts[6], "fsdp", axis=1, tiled=True),
        lax.all_gather(parts[7], "fsdp", axis=0, tiled=True),
        lax.all_gather(parts[8], "fsdp", axis=0, tiled=True),
        lax.all_gather(parts[9], "fsdp", axis=1, tiled=True),
        lax.all_gather(parts[10], "fsdp", axis=1, tiled=True),
        lax.all_gather(parts[11], "fsdp", axis=0, tiled=True),
    )


def reduce_terms(terms):
    shares = (
        lax.psum_scatter(
            terms[0].astype(jnp.bfloat16), "fsdp", scatter_dimension=0, tiled=True
        ).astype(jnp.float32),
        lax.psum_scatter(
            terms[1].astype(jnp.bfloat16), "fsdp", scatter_dimension=0, tiled=True
        ).astype(jnp.float32),
        lax.psum_scatter(
            terms[2].astype(jnp.bfloat16), "fsdp", scatter_dimension=0, tiled=True
        ).astype(jnp.float32),
        lax.psum_scatter(
            terms[3].astype(jnp.bfloat16), "fsdp", scatter_dimension=0, tiled=True
        ).astype(jnp.float32),
        lax.psum_scatter(
            terms[4].astype(jnp.bfloat16), "fsdp", scatter_dimension=1, tiled=True
        ).astype(jnp.float32),
        lax.psum_scatter(
            terms[5].astype(jnp.bfloat16), "fsdp", scatter_dimension=2, tiled=True
        ).astype(jnp.float32),
        lax.psum_scatter(
            terms[6].astype(jnp.bfloat16), "fsdp", scatter_dimension=1, tiled=True
        ).astype(jnp.float32),
        lax.psum_scatter(
            terms[7].astype(jnp.bfloat16), "fsdp", scatter_dimension=0, tiled=True
        ).astype(jnp.float32),
        lax.psum_scatter(
            terms[8].astype(jnp.bfloat16), "fsdp", scatter_dimension=0, tiled=True
        ).astype(jnp.float32),
        lax.psum_scatter(
            terms[9].astype(jnp.bfloat16), "fsdp", scatter_dimension=1, tiled=True
        ).astype(jnp.float32),
        lax.psum_scatter(
            terms[10].astype(jnp.bfloat16), "fsdp", scatter_dimension=1, tiled=True
        ).astype(jnp.float32),
    )
    return (
        lax.psum(shares[0].astype(jnp.bfloat16), "ctx").astype(jnp.float32),
        lax.psum(shares[1].astype(jnp.bfloat16), "ctx").astype(jnp.float32),
        lax.psum(shares[2].astype(jnp.bfloat16), "ctx").astype(jnp.float32),
        lax.psum(shares[3].astype(jnp.bfloat16), "ctx").astype(jnp.float32),
        lax.psum(shares[4].astype(jnp.bfloat16), "ctx").astype(jnp.float32),
        lax.psum(shares[5].astype(jnp.bfloat16), "ctx").astype(jnp.float32),
        lax.psum(shares[6].astype(jnp.bfloat16), "ctx").astype(jnp.float32),
        lax.psum(shares[7].astype(jnp.bfloat16), "ctx").astype(jnp.float32),
        lax.psum(shares[8].astype(jnp.bfloat16), "ctx").astype(jnp.float32),
        lax.psum(shares[9].astype(jnp.bfloat16), "ctx").astype(jnp.float32),
        lax.psum(shares[10].astype(jnp.bfloat16), "ctx").astype(jnp.float32),
    )


def forward_layer(residual, weights, cos_table, sin_table, visible):
    (
        gain_one,
        shift_one,
        gain_two,
        shift_two,
        w_qkv,
        b_qkv,
        w_out,
        b_out,
        w_up,
        b_up,
        w_down,
        b_down,
    ) = weights
    rows_here = residual.shape[0]
    width = w_qkv.shape[2]
    heads_here = width // HD
    normed = layer_norm(
        residual, gain_one.astype(jnp.float32), shift_one.astype(jnp.float32)
    ).astype(jnp.bfloat16)
    mlp_input = layer_norm(
        residual, gain_two.astype(jnp.float32), shift_two.astype(jnp.float32)
    ).astype(jnp.bfloat16)
    projected = jnp.einsum(
        "sd,cdf->csf", normed, w_qkv, preferred_element_type=jnp.float32
    ) + b_qkv.astype(jnp.float32).reshape(3, 1, width)
    query_heads = rotate(
        projected[0].reshape(rows_here, heads_here, HD), cos_table, sin_table
    ).astype(jnp.bfloat16)
    key_turned = (
        rotate(projected[1].reshape(rows_here, heads_here, HD), cos_table, sin_table)
        .astype(jnp.bfloat16)
        .reshape(rows_here, width)
    )
    value_low = projected[2].astype(jnp.bfloat16)
    key_all, value_all = (
        lax.all_gather(key_turned, "ctx", axis=0, tiled=True),
        lax.all_gather(value_low, "ctx", axis=0, tiled=True),
    )
    key_heads = key_all.reshape(-1, heads_here, HD)
    value_heads = value_all.reshape(-1, heads_here, HD)
    scores = score_block(query_heads, key_heads, visible)
    row_max = jnp.max(scores, axis=-1, keepdims=True)
    exp_scores = jnp.exp(scores - row_max)
    row_total = jnp.sum(exp_scores, axis=-1, keepdims=True)
    log_total = row_max + jnp.log(row_total)
    soft_probs = (exp_scores / row_total).astype(jnp.bfloat16)
    attended = (
        jnp.einsum("hst,thd->shd", soft_probs, value_heads, preferred_element_type=jnp.float32)
        .reshape(rows_here, width)
        .astype(jnp.bfloat16)
    )
    pre_act = jnp.dot(mlp_input, w_up, preferred_element_type=jnp.float32) + b_up.astype(
        jnp.float32
    ).reshape(-1)
    activated = jax.nn.gelu(pre_act, approximate=False).astype(jnp.bfloat16)
    partial_value = jnp.dot(attended, w_out, preferred_element_type=jnp.float32) + jnp.dot(
        activated, w_down, preferred_element_type=jnp.float32
    )
    summed = lax.psum(partial_value.astype(jnp.bfloat16), "tp").astype(jnp.float32)
    new_residual = residual + (summed + b_out.astype(jnp.float32) + b_down.astype(jnp.float32))
    saved = (
        normed,
        mlp_input,
        query_heads,
        key_heads,
        value_heads,
        log_total,
        attended,
        pre_act,
        activated,
    )
    return (new_residual, saved)


def backward_layer(grad_residual, residual, weights, saved, cos_table, sin_table, visible):
    (
        gain_one,
        shift_one,
        gain_two,
        shift_two,
        w_qkv,
        b_qkv,
        w_out,
        b_out,
        w_up,
        b_up,
        w_down,
        b_down,
    ) = weights
    (
        normed,
        mlp_input,
        query_heads,
        key_heads,
        value_heads,
        log_total,
        attended,
        pre_act,
        activated,
    ) = saved
    rows_here = residual.shape[0]
    width = w_qkv.shape[2]
    heads_here = width // HD
    score_scale = 1.0 / math.sqrt(HD)
    branch_grad = grad_residual.astype(jnp.bfloat16)
    bias_grad = jnp.sum(branch_grad, axis=0, dtype=jnp.float32)
    grad_w_out = jnp.dot(attended.T, branch_grad, preferred_element_type=jnp.float32)
    grad_w_down = jnp.dot(activated.T, branch_grad, preferred_element_type=jnp.float32)
    grad_attended = jnp.dot(branch_grad, w_out.T, preferred_element_type=jnp.float32).astype(
        jnp.bfloat16
    )
    grad_hidden = jnp.dot(branch_grad, w_down.T, preferred_element_type=jnp.float32)
    gelu_slope = (
        0.5 * (1.0 + lax.erf(pre_act * INV_ROOT_TWO))
        + pre_act * jnp.exp(-0.5 * pre_act * pre_act) * INV_ROOT_TWO_PI
    )
    grad_pre = (grad_hidden * gelu_slope).astype(jnp.bfloat16)
    grad_b_up = jnp.sum(grad_pre, axis=0, dtype=jnp.float32)
    grad_w_up = jnp.dot(mlp_input.T, grad_pre, preferred_element_type=jnp.float32)
    grad_mlp_input = jnp.dot(grad_pre, w_up.T, preferred_element_type=jnp.float32)
    scores = score_block(query_heads, key_heads, visible)
    soft_probs = jnp.exp(scores - log_total)
    grad_att_heads = grad_attended.reshape(rows_here, heads_here, HD)
    grad_probs = jnp.einsum(
        "shd,thd->hst", grad_att_heads, value_heads, preferred_element_type=jnp.float32
    )
    row_dot = jnp.sum(soft_probs * grad_probs, axis=-1, keepdims=True)
    grad_scores = (soft_probs * (grad_probs - row_dot)).astype(jnp.bfloat16)
    grad_query = (
        jnp.einsum("hst,thd->shd", grad_scores, key_heads, preferred_element_type=jnp.float32)
        * score_scale
    )
    grad_keys = (
        jnp.einsum("hst,shd->thd", grad_scores, query_heads, preferred_element_type=jnp.float32)
        * score_scale
    )
    grad_values = jnp.einsum(
        "hst,shd->thd",
        soft_probs.astype(jnp.bfloat16),
        grad_att_heads,
        preferred_element_type=jnp.float32,
    )
    key_part, value_part = (
        lax.psum_scatter(
            grad_keys.reshape(-1, width).astype(jnp.bfloat16),
            "ctx",
            scatter_dimension=0,
            tiled=True,
        ).astype(jnp.float32),
        lax.psum_scatter(
            grad_values.reshape(-1, width).astype(jnp.bfloat16),
            "ctx",
            scatter_dimension=0,
            tiled=True,
        ).astype(jnp.float32),
    )
    back_query = rotate(grad_query, cos_table, -sin_table).reshape(rows_here, width)
    back_key = rotate(key_part.reshape(rows_here, heads_here, HD), cos_table, -sin_table).reshape(
        rows_here, width
    )
    grad_projected = jnp.stack([back_query, back_key, value_part]).astype(jnp.bfloat16)
    grad_b_qkv = jnp.sum(grad_projected, axis=1, dtype=jnp.float32).reshape(3, heads_here, HD)
    grad_w_qkv = jnp.einsum(
        "sd,csf->cdf", normed, grad_projected, preferred_element_type=jnp.float32
    )
    grad_normed = jnp.einsum(
        "csf,cdf->sd", grad_projected, w_qkv, preferred_element_type=jnp.float32
    )
    grad_normed, grad_mlp_input = (
        lax.psum(grad_normed.astype(jnp.bfloat16), "tp").astype(jnp.float32),
        lax.psum(grad_mlp_input.astype(jnp.bfloat16), "tp").astype(jnp.float32),
    )
    unused_one, pull_one = jax.vjp(
        layer_norm, residual, gain_one.astype(jnp.float32), shift_one.astype(jnp.float32)
    )
    back_one, grad_gain_one, grad_shift_one = pull_one(grad_normed)
    unused_two, pull_two = jax.vjp(
        layer_norm, residual, gain_two.astype(jnp.float32), shift_two.astype(jnp.float32)
    )
    back_two, grad_gain_two, grad_shift_two = pull_two(grad_mlp_input)
    grad_before = grad_residual + back_one + back_two
    terms = (
        grad_gain_one,
        grad_shift_one,
        grad_gain_two,
        grad_shift_two,
        grad_w_qkv,
        grad_b_qkv,
        grad_w_out,
        bias_grad,
        grad_w_up,
        grad_b_up.reshape(-1, HD),
        grad_w_down,
    )
    return (grad_before, terms)


def body(
    tokens,
    positions,
    cotangent,
    ln1_gain,
    ln1_bias,
    ln2_gain,
    ln2_bias,
    qkv_weight,
    qkv_bias,
    out_weight,
    out_bias,
    up_weight,
    up_bias,
    down_weight,
    down_bias,
):
    shards = (
        ln1_gain,
        ln1_bias,
        ln2_gain,
        ln2_bias,
        qkv_weight,
        qkv_bias,
        out_weight,
        out_bias,
        up_weight,
        up_bias,
        down_weight,
        down_bias,
    )
    layer_count = ln1_gain.shape[0]
    rows_here = tokens.shape[0]
    seq_len = rows_here * lax.axis_size("ctx")
    query_index = lax.axis_index("ctx") * rows_here + jnp.arange(rows_here, dtype=jnp.int32)
    key_index = jnp.arange(seq_len, dtype=jnp.int32)
    visible = (key_index[None, :] <= query_index[:, None]) & (
        key_index[None, :] >= (query_index - positions)[:, None]
    )
    cos_table, sin_table = turn_tables(positions)
    residual = tokens.astype(jnp.float32)
    weights_kept = []
    layer_at = 0
    weights = gather_layer([stacked[layer_at] for stacked in shards])
    inputs_kept = [residual]
    residual, saved = forward_layer(residual, weights, cos_table, sin_table, visible)
    weights_kept.append(weights)
    saved_kept = [saved]
    output = residual.astype(jnp.bfloat16)
    grad_residual = cotangent.astype(jnp.float32)
    reduced = [None] * layer_count
    for layer_at in reversed(range(layer_count)):
        weights = gather_again([stacked[layer_at] for stacked in shards])
        grad_residual, terms = backward_layer(
            grad_residual,
            inputs_kept[layer_at],
            weights,
            saved_kept[layer_at],
            cos_table,
            sin_table,
            visible,
        )
        reduced[layer_at] = reduce_terms(terms)
    grad_outs = [jnp.stack([reduced[0][member]]) for member in range(11)]
    return (
        output,
        grad_residual,
        grad_outs[0],
        grad_outs[1],
        grad_outs[2],
        grad_outs[3],
        grad_outs[4],
        grad_outs[5],
        grad_outs[6],
        grad_outs[7],
        grad_outs[8],
        grad_outs[9],
        grad_outs[10],
        grad_outs[7],
    )


def solution(mesh):
    in_specs = (
        P(("fsdp", "ctx"), None),
        P(("fsdp", "ctx")),
        P(("fsdp", "ctx"), None),
        P(None, "fsdp"),
        P(None, "fsdp"),
        P(None, "fsdp"),
        P(None, "fsdp"),
        P(None, None, "fsdp", "tp"),
        P(None, None, "tp", "fsdp"),
        P(None, "tp", "fsdp"),
        P(None, "fsdp"),
        P(None, "fsdp", "tp"),
        P(None, "tp", "fsdp"),
        P(None, "tp", "fsdp"),
        P(None, "fsdp"),
    )
    out_specs = (
        P(("fsdp", "ctx"), None),
        P(("fsdp", "ctx"), None),
        P(None, "fsdp"),
        P(None, "fsdp"),
        P(None, "fsdp"),
        P(None, "fsdp"),
        P(None, None, "fsdp", "tp"),
        P(None, None, "tp", "fsdp"),
        P(None, "tp", "fsdp"),
        P(None, "fsdp"),
        P(None, "fsdp", "tp"),
        P(None, "tp", "fsdp"),
        P(None, "tp", "fsdp"),
        P(None, "fsdp"),
    )
    return jax.shard_map(body, mesh=mesh, in_specs=in_specs, out_specs=out_specs, check_vma=False)
```

profile of v0, /device:TPU:1, one launch (start us, length us, event | category | flops | bytes accessed | tf_op | source)
XLA Modules:
  0.0 1518.0 jit_solution(1096871621016568394)
XLA Ops:
  8.1 1.0 convert_reduce_fusion
  9.1 1.1 fusion.49
  10.2 1.3 fusion.72
  12.2 0.9 dynamic-update-slice.2
  13.1 0.8 dynamic-update-slice.3
  13.9 0.8 dynamic-update-slice
  14.8 0.8 dynamic-update-slice.1
  15.6 84.9 %all-reduce.15 = (bf16[512]{0:T(512)(128)(2,1)S(1)}, bf16[512]{0:T(512)(128)(2,1)S(1)}, bf16[512]{0:T(512)(128)(2,1)S(1)}, bf16[512]{0:T(512)(128)(2,1)S(1)}) all-reduce(bf16[512]{0:T(512)(128)(2,1)S(1)} %dynamic-update-slice.1, bf16[512]{0:T(512)(128)(2,1)S(1)} %dynamic-update-slice, ...), channel_id=3, replica_groups=mesh['fsdp'=32,'ctx'=2,'tp'=2] {'fsdp'}, use_global_device_ids=true, to_apply=%add.1 | all-reduce | flops 2048 | bytes 8192
  100.5 0.7 copy.76
  101.2 73.8 %all-gather.3 = bf16[1,3,4,64]{2,1,0,3:T(4,128)(2,1)S(1)} all-gather(bf16[1,3,4,2]{2,1,0,3:T(4,128)(2,1)S(1)} %copy.76), channel_id=5, replica_groups=mesh['fsdp'=32,'ctx'=2,'tp'=2] {'fsdp'}, dimensions={3}, use_global_device_ids=true | all-gather | bytes 1584 | tf_op jit(solution)/shard_map/all_gather | solution.py:66
  175.2 83.6 %all-gather.2 = bf16[1,3,512,256]{3,2,1,0:T(8,128)(2,1)S(1)} all-gather(bf16[1,3,16,256]{3,2,1,0:T(8,128)(2,1)} %param.22), channel_id=4, replica_groups=mesh['fsdp'=32,'ctx'=2,'tp'=2] {'fsdp'}, dimensions={2}, use_global_device_ids=true | all-gather | bytes 811008 | tf_op jit(solution)/shard_map/all_gather | solution.py:65
  259.6 75.9 %all-gather.5 = bf16[1,256,512]{1,2,0:T(8,128)(2,1)S(1)} all-gather(bf16[1,256,16]{1,2,0:T(8,128)(2,1)S(1)} %copy-done.8), channel_id=7, replica_groups=mesh['fsdp'=32,'ctx'=2,'tp'=2] {'fsdp'}, dimensions={2}, use_global_device_ids=true | all-gather | bytes 270336 | tf_op jit(solution)/shard_map/all_gather | solution.py:67
  335.9 58.1 %all-gather.4 = bf16[1,256,256]{2,1,0:T(8,128)(2,1)S(1)} all-gather(bf16[1,128,256]{2,1,0:T(8,128)(2,1)S(1)} %slice.100), channel_id=6, replica_groups=mesh['fsdp'=32,'ctx'=2,'tp'=2] {'ctx'}, dimensions={1}, use_global_device_ids=true | all-gather | bytes 196608 | tf_op jit(solution)/shard_map/all_gather | solution.py:182
  394.3 1.9 all_gather.53
  397.8 0.8 copy.94
  398.9 0.8 copy.84
  399.7 0.5 all-gather.16.cloned.1.call-update
  400.3 0.5 all-gather.18.cloned.1.call-update
  400.9 76.8 %all-gather.9 = bf16[1,16,64]{1,0,2:T(2,128)(2,1)S(1)} all-gather(bf16[1,16,2]{1,0,2:T(2,128)(2,1)S(1)} %copy.81), channel_id=11, replica_groups=mesh['fsdp'=32,'ctx'=2,'tp'=2] {'fsdp'}, dimensions={2}, use_global_device_ids=true | all-gather | bytes 2112 | tf_op jit(solution)/shard_map/all_gather | solution.py:70
  478.5 0.9 copy.95
  479.8 1.3 fusion
  481.1 1.4 copy.88
  482.5 1.0 fusion.6
  483.7 2.6 fusion.17
  486.3 46.4 %all-gather.18.cloned.1.call-done = bf16[1,1024,512]{1,2,0:T(8,128)(2,1)} async-done(((bf16[1,1024,16]{1,2,0:T(8,128)(2,1)}), bf16[1,1024,512]{1,2,0:T(8,128)(2,1)}) %all-gather.18.cloned.1.call-update) | async-done | bytes 1048592 | tf_op jit(solution)/shard_map/all_gather | solution.py:71
  532.7 1.8 fusion.9
  534.5 0.9 fusion.4
  535.4 0.4 fusion.74
  535.8 0.8 copy-done.5
  536.6 1.1 convolution_convert_fusion.4
  537.8 1.0 convolution_convert_fusion.3
  538.9 1.5 convolution_convert_fusion.1
  542.4 1.5 convolution_convert_fusion
  544.2 321.3 %all-reduce.22.cloned.1.call-done = bf16[3,512,256]{2,0,1:T(4,128)(2,1)} async-done(((bf16[3,512,256]{2,0,1:T(4,128)(2,1)}), bf16[3,512,256]{2,0,1:T(4,128)(2,1)}) %all-reduce.22.cloned.1.call-update) | async-done | bytes 786448
  865.5 1.4 dynamic-slice_bitcast_fusion
  867.0 56.8 %all-reduce.24.cloned.1.call-done = (bf16[128,512]{1,0:T(8,128)(2,1)}, bf16[128,512]{1,0:T(8,128)(2,1)}, bf16[128,512]{1,0:T(8,128)(2,1)}) async-done(((bf16[128,512]{1,0:T(8,128)(2,1)}, bf16[128,512]{1,0:T(8,128)(2,1)}, bf16[128,512]{1,0:T(8,128)(2,1)}), (bf16[128,512]{1,0:T(8,128)(2,1)}, bf16[128,512]{1,0:T(8,128)(2,1)}, bf16[128,512]{1,0:T(8,128)(2,1)})) %all-reduce.24.cloned.1.call-update) | async-done | bytes 393232 | tf_op jit(solution)/shard_map/psum | solution.py:204
  923.8 1.0 reduce_sum.176
  924.8 0.9 reduce_sum.174
  925.7 1.2 fusion.50
  926.9 1.3 fusion.48
  928.2 158.7 %all-reduce.14 = (bf16[512]{0:T(512)(128)(2,1)S(1)}, bf16[512]{0:T(512)(128)(2,1)S(1)}, bf16[512]{0:T(512)(128)(2,1)S(1)}, bf16[512]{0:T(512)(128)(2,1)S(1)}, bf...) all-reduce(bf16[512]{0:T(512)(128)(2,1)S(1)} %dynamic-update-slice., ...), channel_id=14, replica_groups=mesh['fsdp'=32,'ctx'=2,'tp'=2] {'fsdp'}, use_global_device_ids=true, to_apply=%add.5 | all-reduce | flops 5376 | bytes 21504
  1087.0 0.6 copy.91
  1087.6 0.6 copy.98
  1088.2 0.6 dynamic-slice_bitcast_fusion.5
  1088.8 0.6 dynamic-slice_bitcast_fusion.4
  1089.3 0.6 dynamic-slice_bitcast_fusion.3
  1089.9 0.6 dynamic-slice_bitcast_fusion.2
  1090.5 0.6 dynamic-slice_bitcast_fusion.1
  1091.1 179.7 %reduce-scatter.13.cloned.1.call-done = bf16[16,1024]{1,0:T(8,128)(2,1)} async-done(((bf16[512,1024]{1,0:T(8,128)(2,1)}), bf16[16,1024]{1,0:T(8,128)(2,1)}) %reduce-scatter.13.cloned.1.call-update) | async-done | bytes 32784 | tf_op jit(solution)/shard_map/reduce_scatter | solution.py:119
  1270.8 182.6 %reduce-scatter.15.cloned.1.call-done = bf16[1024,16]{0,1:T(8,128)(2,1)} async-done(((bf16[1024,512]{0,1:T(8,128)(2,1)}), bf16[1024,16]{0,1:T(8,128)(2,1)}) %reduce-scatter.15.cloned.1.call-update) | async-done | bytes 32784 | tf_op jit(solution)/shard_map/reduce_scatter | solution.py:125
  1453.4 1.0 add_add_fusion.2
  1454.4 42.9 %all-reduce.26.cloned.1.call-done = (bf16[1,3,16,256]{3,1,2,0:T(4,128)(2,1)}, bf16[1,16]{1,0:T(2,128)(2,1)}, bf16[1,16]{1,0:T(2,128)(2,1)}, bf16[1,16]{1,0:T(2,1...) async-done(((bf16[1,3,16,256]{3,1,2,0:T(4,128)(2,1)}, ...) | async-done | bytes 98592 | tf_op jit(solution)/shard_map/psum | solution.py:134
  1497.2 0.7 stack.91
  1497.9 1.1 stack.77
  1499.0 1.2 stack.79
  1500.1 1.2 stack.81
  1501.3 1.1 stack.83
  1502.4 1.2 stack.95
  1503.6 1.3 stack.87
  1504.8 1.4 copy.92
  1506.2 1.3 stack.89
  1507.5 1.4 stack.93
  1508.9 1.4 stack.97
  1510.3 0.5 copy.124
  (114 shorter events, 6.1 us)
Async XLA Ops:
  8.0 250.8 %copy-start = (bf16[128,512]{1,0:T(8,128)(2,1)S(1)}, bf16[128,512]{1,0:T(8,128)(2,1)}, u32[]{:S(2)}) copy-start(bf16[128,512]{1,0:T(8,128)(2,1)} %param.15) | copy-start | bytes 393220
  8.0 470.4 %reduce-scatter.17.cloned.1.call-start = ((), (), s32[]{:S(2)}) async-start(), calls=%async_computation.11 | async-start | bytes 196608
  258.9 0.7 copy-start.9
  258.9 0.7 copy-start.8
  258.9 76.6 %copy-start.1 = (bf16[128,512]{1,0:T(8,128)(2,1)S(1)}, bf16[128,512]{1,0:T(8,128)(2,1)}, u32[]{:S(2)}) copy-start(bf16[128,512]{1,0:T(8,128)(2,1)} %param.17) | copy-start | bytes 393220
  397.6 3.3 copy-start.10
  398.6 81.2 %reduce-scatter.9.cloned.1.call-start = ((), (), s32[]{:S(2)}) async-start(), calls=%async_computation.5 | async-start | bytes 196608 | tf_op jit(solution)/shard_map/reduce_scatter | solution.py:295
  399.7 84.0 %all-gather.16.cloned.1.call-start = ((), (), s32[]{:S(2)}) async-start(), calls=%async_computation.9 | async-start | bytes 1081344 | tf_op jit(solution)/shard_map/all_gather | solution.py:69
  400.3 132.4 %all-gather.18.cloned.1.call-start = ((), (), s32[]{:S(2)}) async-start(), calls=%async_computation.10 | async-start | bytes 1081344 | tf_op jit(solution)/shard_map/all_gather | solution.py:71
  400.8 464.6 %all-reduce.22.cloned.1.call-start = ((), (), s32[]{:S(2)}) async-start(), calls=%async_computation.12 | async-start | bytes 2097152
  481.1 1.4 copy-start.7
  483.6 440.2 %all-reduce.24.cloned.1.call-start = ((), (), s32[]{:S(2)}) async-start(), calls=%async_computation.13 | async-start | bytes 786432 | tf_op jit(solution)/shard_map/psum | solution.py:204
  532.7 2.7 copy-start.4
  535.4 1.2 copy-start.5
  537.8 553.3 %reduce-scatter.11.cloned.1.call-start = ((), (), s32[]{:S(2)}) async-start(), calls=%async_computation.6 | async-start | bytes 270336 | tf_op jit(solution)/shard_map/reduce_scatter | solution.py:113
  538.8 3.0 copy-start.11
  538.8 3.3 copy-start.12
  538.9 731.9 %reduce-scatter.13.cloned.1.call-start = ((), (), s32[]{:S(2)}) async-start(), calls=%async_computation.7 | async-start | bytes 1081344 | tf_op jit(solution)/shard_map/reduce_scatter | solution.py:119
  540.5 912.9 %reduce-scatter.15.cloned.1.call-start = ((), (), s32[]{:S(2)}) async-start(), calls=%async_computation.8 | async-start | bytes 1081344 | tf_op jit(solution)/shard_map/reduce_scatter | solution.py:125
  543.9 953.4 %all-reduce.26.cloned.1.call-start = ((), (), s32[]{:S(2)}) async-start(), calls=%async_computation.14 | async-start | bytes 222208 | tf_op jit(solution)/shard_map/psum | solution.py:134
  923.8 529.6 %copy-start.2 = (bf16[128,512]{1,0:T(8,128)(2,1)S(1)}, bf16[128,512]{1,0:T(8,128)(2,1)}, u32[]{:S(2)}) copy-start(bf16[128,512]{1,0:T(8,128)(2,1)} %get-tuple-element.92) | copy-start | bytes 393220
  923.8 529.6 %copy-start.3 = (bf16[128,512]{1,0:T(8,128)(2,1)S(1)}, bf16[128,512]{1,0:T(8,128)(2,1)}, u32[]{:S(2)}) copy-start(bf16[128,512]{1,0:T(8,128)(2,1)} %get-tuple-element.93) | copy-start | bytes 393220
  923.8 529.6 %copy-start.6 = (bf16[128,512]{1,0:T(8,128)(2,1)S(1)}, bf16[128,512]{1,0:T(8,128)(2,1)}, u32[]{:S(2)}) copy-start(bf16[128,512]{1,0:T(8,128)(2,1)} %get-tuple-element.91) | copy-start | bytes 393220
  1497.9 13.0 copy-start.13
Sparse Core Ops, SparseCore 0:
  398.7 7.0 reduce-scatter.16
  408.7 11.5 reduce-scatter.8
  1453.5 43.6 all-reduce.25
Sparse Core Ops, SparseCore 1:
  403.3 62.0 all-gather.15
  468.4 64.2 all-gather.17
  535.0 330.4 all-reduce.21
  868.9 54.8 all-reduce.23
  926.7 159.3 reduce-scatter.10
  1088.6 182.2 reduce-scatter.12
  1273.0 180.3 reduce-scatter.14
where the time goes:
time: 1520 us
  waiting for transfers between devices  831 us (55%)
  blocking collectives  614 us (40%)
  other arithmetic  20.1 us (1%)
  local copies, waits for them, and re-layouts  19.7 us (1%)
  between operations  17.7 us (1%)
  matrix products  15.5 us (1%)
    unnamed x12, waiting for transfers between devices  322 us
    unnamed x2, blocking collectives  244 us
    reduce_scatter x1, waiting for transfers between devices, reduce_terms(): lax.psum_scatter(terms[10].astype(jnp.bfloat16), 'fsdp', scatter_dimensio...  183 us
    reduce_scatter x1, waiting for transfers between devices, reduce_terms(): lax.psum_scatter(terms[8].astype(jnp.bfloat16), 'fsdp', scatter_dimension...  180 us
    all_gather x1, blocking collectives, gather_layer(): lax.all_gather(parts[4], 'fsdp', axis=1, tiled=True)  83.6 us
    all_gather x1, blocking collectives, gather_layer(): lax.all_gather(parts[9], 'fsdp', axis=1, tiled=True)  76.8 us
    all_gather x1, blocking collectives, gather_layer(): lax.all_gather(parts[6], 'fsdp', axis=1, tiled=True)  75.9 us
    all_gather x1, blocking collectives, gather_layer(): lax.all_gather(parts[5], 'fsdp', axis=2, tiled=True)  73.8 us
  transfers between devices with their start and end apart: 10, of which 6 were waited for; matrix products, arithmetic and copies ran while one was open for 2% of the time, Pallas kernels for 0%

commit v1 on v0

v1 whole, which is shorter than its diff:
```python
import math

import jax
import jax.numpy as jnp
import numpy as np
from jax import lax
from jax.experimental import pallas as pl
from jax.experimental.pallas import tpu as pltpu
from jax.sharding import PartitionSpec as P

HD = 64
ROT = 16
EPS = 1e-05
BASE = 10000.0
MASKED = -1e30
SCALE = 1.0 / math.sqrt(HD)
INV_ROOT_TWO = 1.0 / math.sqrt(2.0)
INV_ROOT_TWO_PI = 1.0 / math.sqrt(2.0 * math.pi)
MESH = pl.DeviceIdType.MESH
F32 = jnp.float32
BF16 = jnp.bfloat16

UP = slice(0, 256)
QK = slice(256, 384)
DN = slice(384, 640)
VO = slice(640, 768)
HALF = (slice(0, 384), slice(384, 768))

M_XW, M_XE = 0, 1
M_POS = 2
M_TOK = 5
M_COT = 8
M_AG1 = 12
M_AGE1 = 18
M_AG2 = 21
M_AGE2 = 27
M_OUT = 30
M_DX = 34
M_RS1 = 38
M_RSE1 = 44
M_RS2 = 47
M_RSE2 = 53
M_FIN = 56
M_FINE = 59
M_ALL = 66


def dot_nn(left, right):
    return lax.dot_general(left, right, (((1,), (0,)), ((), ())), preferred_element_type=F32)


def dot_nt(left, right):
    return lax.dot_general(left, right, (((1,), (1,)), ((), ())), preferred_element_type=F32)


def dot_tn(left, right):
    return lax.dot_general(left, right, (((0,), (0,)), ((), ())), preferred_element_type=F32)


def iota(shape, dim):
    return lax.broadcasted_iota(jnp.int32, shape, dim)


def turn_partner(pair):
    lane = iota(pair.shape, 1) % HD
    return jnp.where(
        lane < ROT // 2, pltpu.roll(pair, pair.shape[1] - ROT // 2, 1), pltpu.roll(pair, ROT // 2, 1)
    )


def kernel(
    tok_in, pos_in, cot_in, gain1, shift1, gain2, shift2, qkv_w, qkv_b, out_w, out_b, up_w, up_b, down_w, down_b,
    out_o, gin_o, gg1_o, gb1_o, gg2_o, gb2_o, gqkvw_o, gqkvb_o, goutw_o, gbias_o, gupw_o, gupb_o, gdownw_o,
    W, XS, E, XE, TK, CT, PS, SM,
    NRM, RSQ, NB, MB, NTR, MTR, BTR, COS, SIN, PCOL,
    GC, GVZ, ATZ, PO, RO, SO, XO, PD, RD, SD, XD,
    GS, RA1, RB1, SA, SB, RA2, RB2, EG, RE1, SE, RE2, FB, XR, FE, XF,
    ss, rs,
):
    place = lax.axis_index("fsdp")
    z, y, xh = place // 8, (place // 2) % 4, place % 2
    c = lax.axis_index("ctx")
    t = lax.axis_index("tp")
    ox, oc, ot = 1 - xh, 1 - c, 1 - t

    def dev(xx, cc, tt, zz=z, yy=y):
        return {"fsdp": zz * 8 + yy * 2 + xx, "ctx": cc, "tp": tt}

    def zdev(k):
        return dev(xh, c, t, zz=(z + k) % 4)

    def ydev(k):
        return dev(xh, c, t, yy=(y + k) % 4)

    def send(number, src, dst, where):
        copy = pltpu.make_async_remote_copy(
            src_ref=src, dst_ref=dst, send_sem=ss.at[number], recv_sem=rs.at[number],
            device_id=where, device_id_type=MESH,
        )
        copy.start()
        return copy

    sent = []

    def track(copy):
        sent.append(copy)
        return copy

    barrier = pltpu.get_barrier_semaphore()
    group = [
        dev(xh, oc, t), dev(ox, c, t), dev(ox, c, ot), dev(ox, oc, t), dev(xh, c, ot), dev(xh, oc, ot), dev(ox, oc, ot)
    ]
    peers = group + [zdev(k) for k in (1, 2, 3)] + [ydev(k) for k in (1, 2, 3)]
    for peer in peers:
        pl.semaphore_signal(barrier, inc=1, device_id=peer, device_id_type=MESH)

    def cut(xx):
        lanes = pl.ds(pl.multiple_of(xx * 128, 128), 128)
        q_pair, k_pair, v_pair, o_pair = (
            ref[:, lanes].astype(F32) for ref in (qkv_w.at[0], qkv_w.at[1], qkv_w.at[2], out_w)
        )
        low = iota((16, 128), 1) < HD
        first = c == 0

        def halves(a, b):
            a_low = jnp.where(first, a, pltpu.roll(a, HD, 1))
            b_high = jnp.where(first, pltpu.roll(b, HD, 1), b)
            return jnp.where(low, a_low, b_high).astype(BF16)

        wide = pl.ds(pl.multiple_of((xx * 2 + c) * 256, 256), 256)
        return up_w[:, wide], halves(q_pair, k_pair), down_w[:, wide], halves(v_pair, o_pair)

    for target, xx in ((XS, ox), (W.at[z, y, xh], xh)):
        up_cut, qk_cut, down_cut, vo_cut = cut(xx)
        target[:, UP] = up_cut
        target[:, QK] = qk_cut
        target[:, DN] = down_cut
        target[:, VO] = vo_cut

    SM[...] = jnp.zeros((16, 128), F32)
    for row, ref in enumerate((gain1, shift1, gain2, shift2, out_b, down_b)):
        SM[row : row + 1, 0:16] = ref[...].astype(F32)
    for which in range(3):
        SM[8 + 2 * which : 10 + 2 * which, 0:4] = qkv_b[which].astype(F32)
    SM[6:8, 0:16] = up_b[...].astype(F32)
    SM[14:16, 0:16] = up_b[...].astype(F32)

    row16, lane16 = iota((16, 128), 0), iota((16, 128), 1)

    def placed(xx):
        raw = SM[...]
        head = xx * 2 + c

        def column(lane):
            return jnp.sum(jnp.where(lane16 == lane, raw, 0.0), axis=1, keepdims=True)

        spread = pltpu.roll(raw, 16 * (y * 2 + xh), 1)
        low = lane16 < HD
        hit = (lane16 % HD) == 2 * place + row16 % 2
        qkv = jnp.where(low != ((row16 == 10) | (row16 == 11)), column(head), 0.0)
        up_first = jnp.where(low, column(4 * head), column(4 * head + 1))
        up_second = jnp.where(low, column(4 * head + 2), column(4 * head + 3))
        bias = jnp.where(row16 < 8, up_first, jnp.where(row16 < 14, qkv, up_second))
        return jnp.where(row16 < 6, spread, jnp.where(hit, bias, 0.0))

    XE[0] = placed(ox).astype(BF16)
    XE[1] = placed(xh).astype(BF16)

    TK[xh, c] = tok_in[...]
    CT[xh, c] = cot_in[...]
    PS[xh, c] = pos_in[...]

    pl.semaphore_wait(barrier, len(peers))

    xw = track(send(M_XW, XS, W.at[z, y, xh], dev(ox, c, t)))
    xe = track(send(M_XE, XE.at[0], XE.at[2], dev(ox, c, t)))
    across = dev(ox, c, ot)
    core = dev(xh, oc, t)
    tok_across = track(send(M_TOK, tok_in, TK.at[xh, c], across))
    tok_core = track(send(M_TOK + 1, tok_in, TK.at[xh, c], core))
    pos_copies = [
        track(send(M_POS + i, pos_in, PS.at[xh, c], where))
        for i, where in enumerate((core, dev(ox, c, t), dev(ox, oc, t)))
    ]
    cot_across = track(send(M_COT, cot_in, CT.at[xh, c], across))
    cot_core = track(send(M_COT + 1, cot_in, CT.at[xh, c], core))

    xw.wait_recv()
    ag1 = []
    for k in (2, 1, 3):
        here = W.at[z, y, :, :, HALF[0]]
        ag1.append(track(send(M_AG1 + k - 1, here, here, zdev(k))))
        here = W.at[z, y, :, :, HALF[1]]
        ag1.append(track(send(M_AG1 + 3 + k - 1, here, here, ydev(k))))
    xe.wait_recv()
    E[z, y] = (XE[1].astype(F32) + XE[2].astype(F32)).astype(BF16)
    for k in (2, 1, 3):
        ag1.append(track(send(M_AGE1 + k - 1, E.at[z, y], E.at[z, y], zdev(k))))
    tok_across.wait_recv()
    tok_pass = track(send(M_TOK + 2, TK.at[ox, c], TK.at[ox, c], core))
    for copy in ag1:
        copy.wait_recv()
    ag2 = []
    age2 = []
    for k in (2, 1, 3):
        age2.append(track(send(M_AGE2 + k - 1, E.at[:, y], E.at[:, y], ydev(k))))
    for k in (2, 1, 3):
        here = W.at[:, y, :, :, HALF[0]]
        ag2.append(track(send(M_AG2 + k - 1, here, here, ydev(k))))
        here = W.at[z, :, :, :, HALF[1]]
        ag2.append(track(send(M_AG2 + 3 + k - 1, here, here, zdev(k))))
    cot_across.wait_recv()
    cot_pass = track(send(M_COT + 2, CT.at[ox, c], CT.at[ox, c], core))
    tok_core.wait_recv()
    tok_pass.wait_recv()

    for s in range(2):
        rows = TK[s].reshape(256, 512).astype(F32)
        centered = rows - jnp.mean(rows, axis=1, keepdims=True)
        moment = jnp.mean(centered * centered, axis=1, keepdims=True)
        rsq = lax.rsqrt(moment + EPS)
        NRM[s] = centered * rsq
        RSQ[s] = jnp.broadcast_to(rsq, (256, 128))

    for copy in pos_copies:
        copy.wait_recv()
    row8 = iota((8, 128), 0)
    inverse = jnp.zeros((8, 128), F32)
    for r in range(ROT // 2):
        inverse = jnp.where(row8 == r, float(np.float32(BASE ** (-2.0 * r / ROT))), inverse)
    ones, zeros = jnp.ones((48, 128), F32), jnp.zeros((48, 128), F32)
    for s in range(2):
        for b in range(2):
            places = PS[s, b].astype(F32)
            angle = jnp.broadcast_to(places, (8, 128)) * inverse
            cos, sin = jnp.cos(angle), jnp.sin(angle)
            part = pl.ds(b * 128, 128)
            COS[s, part] = jnp.concatenate([cos, cos, ones, cos, cos, ones], axis=0).T
            SIN[s, part] = jnp.concatenate([-sin, sin, zeros, -sin, sin, zeros], axis=0).T
            PCOL[s, part] = jnp.broadcast_to(places, (128, 128)).T

    cot_core.wait_recv()
    cot_pass.wait_recv()
    bias_grad = jnp.zeros((1, 512), F32)
    for s in range(2):
        grad = CT[s].reshape(256, 512)
        BTR[:, s * 256 : (s + 1) * 256] = grad.T
        bias_grad = bias_grad + jnp.sum(grad.astype(F32), axis=0, keepdims=True)

    for copy in age2:
        copy.wait_recv()
    per_z = []
    for zz in range(4):
        total = E[zz, 0].astype(F32)
        for yy in range(1, 4):
            total = total + E[zz, yy].astype(F32)
        per_z.append(total)
    vectors = jnp.concatenate(per_z, axis=1)
    all_z = per_z[0] + per_z[1] + per_z[2] + per_z[3]
    g1, b1, g2, b2 = (vectors[r : r + 1] for r in range(4))
    b_branch = vectors[4:5] + vectors[5:6]
    b_up = jnp.concatenate([all_z[6:7] + all_z[7:8], all_z[14:15] + all_z[15:16]], axis=1)
    b_qk = all_z[8:9] + all_z[9:10] + all_z[10:11] + all_z[11:12]
    b_v = (all_z[12:13] + all_z[13:14])[:, :HD]

    for s in range(2):
        n = NRM[s]
        normed = (n * g1 + b1).astype(BF16)
        mlp_input = (n * g2 + b2).astype(BF16)
        NB[s] = normed
        MB[s] = mlp_input
        NTR[:, s * 256 : (s + 1) * 256] = normed.T
        MTR[:, s * 256 : (s + 1) * 256] = mlp_input.T

    for copy in ag2:
        copy.wait_recv()

    gb_up = jnp.zeros((1, 256), F32)
    gb_qk = jnp.zeros((1, 128), F32)
    gb_v = jnp.zeros((1, HD), F32)
    for s in range(2):
        part = slice(s * 256, (s + 1) * 256)
        normed, mlp_input, branch_grad = NB[s], MB[s], CT[s].reshape(256, 512)
        w_up = W[:, :, :, :, UP].reshape(512, 256)
        w_down = W[:, :, :, :, DN].reshape(512, 256)
        w_qk = W[:, :, :, :, QK].reshape(512, 128)
        w_vo = W[:, :, :, :, VO].reshape(512, 128)
        pre_act = dot_nn(mlp_input, w_up) + b_up
        phi = 0.5 * (1.0 + lax.erf(pre_act * INV_ROOT_TWO))
        density = jnp.exp(-0.5 * pre_act * pre_act) * INV_ROOT_TWO_PI
        activated = (pre_act * phi).astype(BF16)
        grad_pre = (dot_nn(branch_grad, w_down) * (phi + pre_act * density)).astype(BF16)
        gb_up = gb_up + jnp.sum(grad_pre.astype(F32), axis=0, keepdims=True)
        GC[part, UP] = grad_pre
        GC[part, DN] = activated

        cos, sin = COS[s], SIN[s]
        qk = dot_nn(normed, w_qk) + b_qk
        qk = (qk * cos + turn_partner(qk) * sin).astype(BF16)
        query, key = qk[:, :HD], qk[:, HD:]
        value = (dot_nn(normed, w_vo)[:, :HD] + b_v).astype(BF16)
        grad_att = dot_nn(branch_grad, w_vo)[:, HD:].astype(BF16)
        row, col = iota((256, 256), 0), iota((256, 256), 1)
        start = row.astype(F32) - jnp.concatenate([PCOL[s], PCOL[s]], axis=1)
        visible = (col <= row) & (col.astype(F32) >= start)
        scores = jnp.where(visible, dot_nt(query, key) * SCALE, MASKED)
        exps = jnp.exp(scores - jnp.max(scores, axis=1, keepdims=True))
        probs = exps / jnp.sum(exps, axis=1, keepdims=True)
        probs_low = probs.astype(BF16)
        attended = dot_nn(probs_low, value).astype(BF16)
        grad_probs = dot_nt(grad_att, value)
        row_dot = jnp.sum(probs * grad_probs, axis=1, keepdims=True)
        grad_scores = (probs * (grad_probs - row_dot)).astype(BF16)
        grad_query = dot_nn(grad_scores, key) * SCALE
        grad_key = dot_tn(grad_scores, query) * SCALE
        grad_value = dot_tn(probs_low, grad_att).astype(BF16)
        grad_qk = jnp.concatenate([grad_query, grad_key], axis=1)
        grad_qk = (grad_qk * cos - turn_partner(grad_qk) * sin).astype(BF16)
        gb_qk = gb_qk + jnp.sum(grad_qk.astype(F32), axis=0, keepdims=True)
        gb_v = gb_v + jnp.sum(grad_value.astype(F32), axis=0, keepdims=True)
        blank = jnp.zeros((256, HD), BF16)
        GC[part, QK] = grad_qk
        GVZ[part] = jnp.concatenate([grad_value, blank], axis=1)
        ATZ[part] = jnp.concatenate([blank, attended], axis=1)
        branch = dot_nt(activated, w_down) + dot_nt(ATZ[part], w_vo)
        PO[s] = branch.astype(BF16).reshape(2, 128, 512)

    out_core = track(send(M_OUT, PO.at[:, oc], RO, core))

    GS[:, :, :, UP] = dot_nn(MTR[...], GC[:, UP]).astype(BF16).reshape(4, 4, 32, 256)
    GS[:, :, :, QK] = dot_nn(NTR[...], GC[:, QK]).astype(BF16).reshape(4, 4, 32, 128)
    rs1 = []
    for k in (2, 1, 3):
        rs1.append(track(send(M_RS1 + k - 1, GS.at[:, (y + k) % 4, :, HALF[0]], RA1.at[k - 1], ydev(k))))
    GS[:, :, :, DN] = dot_nn(BTR[...], GC[:, DN]).astype(BF16).reshape(4, 4, 32, 256)
    grad_vo = dot_nn(NTR[...], GVZ[...]) + dot_nn(BTR[...], ATZ[...])
    GS[:, :, :, VO] = grad_vo.astype(BF16).reshape(4, 4, 32, 128)
    for k in (2, 1, 3):
        rs1.append(track(send(M_RS1 + 3 + k - 1, GS.at[(z + k) % 4, :, :, HALF[1]], RB1.at[k - 1], zdev(k))))

    out_core.wait_recv()
    SO[...] = (PO[:, c].astype(F32) + RO[...].astype(F32)).astype(BF16)
    out_copies = [
        track(send(M_OUT + 1, SO.at[ox], XO.at[0], dev(ox, c, ot))),
        track(send(M_OUT + 2, SO.at[ox], XO.at[1], dev(ox, c, t))),
        track(send(M_OUT + 3, SO.at[xh], XO.at[2], dev(xh, c, ot))),
    ]

    totals = [jnp.zeros((1, 512), F32) for _ in range(4)]
    for s in range(2):
        part = slice(s * 256, (s + 1) * 256)
        w_up = W[:, :, :, :, UP].reshape(512, 256)
        w_qk = W[:, :, :, :, QK].reshape(512, 128)
        w_vo = W[:, :, :, :, VO].reshape(512, 128)
        n = NRM[s]
        grad_mlp = dot_nt(GC[part, UP], w_up)
        grad_normed = dot_nt(GC[part, QK], w_qk) + dot_nt(GVZ[part], w_vo)
        for i, term in enumerate((grad_normed * n, grad_normed, grad_mlp * n, grad_mlp)):
            totals[i] = totals[i] + jnp.sum(term, axis=0, keepdims=True)
        joined = grad_normed * g1 + grad_mlp * g2
        mean_one = jnp.mean(joined, axis=1, keepdims=True)
        mean_two = jnp.mean(joined * n, axis=1, keepdims=True)
        term = RSQ[s][:, :1] * (joined - mean_one - n * mean_two)
        PD[s] = term.astype(BF16).reshape(2, 128, 512)
    dx_core = track(send(M_DX, PD.at[:, oc], RD, core))

    up_rows = jnp.concatenate([gb_up[:, :128], gb_up[:, 128:]], axis=0)
    v_row = jnp.concatenate([gb_v, jnp.zeros((1, 128 - HD), F32)], axis=1)
    for zz in range(4):
        lanes = slice(zz * 128, (zz + 1) * 128)
        pieces = [total[:, lanes] for total in totals] + [bias_grad[:, lanes], gb_qk, v_row, up_rows]
        EG[zz] = jnp.concatenate(pieces + [jnp.zeros((7, 128), F32)], axis=0).astype(BF16)
    rse1 = [track(send(M_RSE1 + k - 1, EG, RE1.at[k - 1], ydev(k))) for k in (2, 1, 3)]

    dx_core.wait_recv()
    SD[...] = (PD[:, c].astype(F32) + RD[...].astype(F32)).astype(BF16)
    dx_copies = [
        track(send(M_DX + 1, SD.at[ox], XD.at[0], dev(ox, c, ot))),
        track(send(M_DX + 2, SD.at[ox], XD.at[1], dev(ox, c, t))),
        track(send(M_DX + 3, SD.at[xh], XD.at[2], dev(xh, c, ot))),
    ]

    for copy in rs1:
        copy.wait_recv()

    def summed(own, received):
        total = own.astype(F32)
        for k in range(3):
            total = total + received[k].astype(F32)
        return total

    SA[...] = summed(GS[:, y, :, HALF[0]], RA1).astype(BF16)
    rs2 = [track(send(M_RS2 + k - 1, SA.at[(z + k) % 4], RA2.at[k - 1], zdev(k))) for k in (2, 1, 3)]
    SB[...] = summed(GS[z, :, :, HALF[1]], RB1).astype(BF16)
    rs2 += [track(send(M_RS2 + 3 + k - 1, SB.at[(y + k) % 4], RB2.at[k - 1], ydev(k))) for k in (2, 1, 3)]
    for copy in rse1:
        copy.wait_recv()
    SE[...] = summed(EG[...], RE1).astype(BF16)
    rse2 = [track(send(M_RSE2 + k - 1, SE.at[(z + k) % 4], RE2.at[k - 1], zdev(k))) for k in (2, 1, 3)]

    def over_chips(own, received):
        return (own.astype(F32) + received[2].astype(F32)) + (received[0].astype(F32) + received[1].astype(F32))

    for copy in out_copies:
        copy.wait_recv()
    out_o[...] = (tok_in[...].astype(F32) + (over_chips(SO[xh], XO) + b_branch)).astype(BF16)
    for copy in dx_copies:
        copy.wait_recv()
    gin_o[...] = cot_in[...].astype(F32) + over_chips(SD[xh], XD)

    for copy in rs2:
        copy.wait_recv()
    FB[:, :, HALF[0]] = summed(SA[z], RA2).astype(BF16).reshape(2, 16, 384)
    FB[:, :, HALF[1]] = summed(SB[y], RB2).astype(BF16).reshape(2, 16, 384)
    fin = [
        track(send(M_FIN, FB.at[ox], XR.at[xh, c], dev(ox, c, t))),
        track(send(M_FIN + 1, FB.at[ox], XR.at[xh, c], dev(ox, oc, t))),
        track(send(M_FIN + 2, FB.at[xh], XR.at[xh, c], dev(xh, oc, t))),
    ]
    XR[xh, c] = FB[xh]
    for copy in rse2:
        copy.wait_recv()
    FE[...] = summed(SE[z], RE2).astype(BF16)
    fine = [track(send(M_FINE + i, FE, XF.at[t, xh, c], where)) for i, where in enumerate(group)]
    XF[t, xh, c] = FE[...]

    for copy in fin:
        copy.wait_recv()
    for xx in range(2):
        both = [XR[xx, 0].astype(F32), XR[xx, 1].astype(F32)]
        lanes = slice(xx * 128, (xx + 1) * 128)
        low = iota((16, 128), 1) < HD

        def join(first, second):
            return jnp.where(low, first, pltpu.roll(second, HD, 1)), jnp.where(low, pltpu.roll(first, HD, 1), second)

        q_new, k_new = join(both[0][:, QK], both[1][:, QK])
        v_new, o_new = join(both[0][:, VO], both[1][:, VO])
        gqkvw_o[0, :, lanes] = q_new
        gqkvw_o[1, :, lanes] = k_new
        gqkvw_o[2, :, lanes] = v_new
        goutw_o[:, lanes] = o_new
        for cc in range(2):
            wide = slice((xx * 2 + cc) * 256, (xx * 2 + cc + 1) * 256)
            gupw_o[:, wide] = both[cc][:, UP]
            gdownw_o[:, wide] = both[cc][:, DN]

    for copy in fine:
        copy.wait_recv()
    tiles = [[[XF[tt, xx, cc].astype(F32) for cc in range(2)] for xx in range(2)] for tt in range(2)]
    whole = jnp.zeros((16, 128), F32)
    for tt in range(2):
        for xx in range(2):
            for cc in range(2):
                whole = whole + tiles[tt][xx][cc]
    whole = jnp.where(row16 == 4, tiles[0][0][0], whole)
    whole = pltpu.roll(whole, (128 - 16 * (y * 2 + xh)) % 128, 1)
    for row, ref in enumerate((gg1_o, gb1_o, gg2_o, gb2_o, gbias_o)):
        ref[...] = whole[row : row + 1, 0:16]
    j4, h4 = iota((2, 4), 0), iota((2, 4), 1)
    j16, h16 = iota((2, 16), 0), iota((2, 16), 1)
    new_qkv = [jnp.zeros((2, 4), F32) for _ in range(3)]
    new_up = jnp.zeros((2, 16), F32)
    for xx in range(2):
        for cc in range(2):
            head = xx * 2 + cc
            tile = jnp.where(t == 0, tiles[0][xx][cc], tiles[1][xx][cc])
            for j in range(2):
                low_col = jnp.sum(jnp.where(lane16 == 2 * place + j, tile, 0.0), axis=1, keepdims=True)
                high_col = jnp.sum(jnp.where(lane16 == HD + 2 * place + j, tile, 0.0), axis=1, keepdims=True)
                spot = (j4 == j) & (h4 == head)
                for which, item in enumerate((low_col[5:6], high_col[5:6], low_col[6:7])):
                    new_qkv[which] = jnp.where(spot, item, new_qkv[which])
                for u, item in enumerate((low_col[7:8], high_col[7:8], low_col[8:9], high_col[8:9])):
                    new_up = jnp.where((j16 == j) & (h16 == head * 4 + u), item, new_up)
    for which in range(3):
        gqkvb_o[which] = new_qkv[which]
    gupb_o[...] = new_up

    for copy in sent:
        copy.wait_send()


def body(
    tokens, positions, cotangent, ln1_gain, ln1_bias, ln2_gain, ln2_bias, qkv_weight, qkv_bias, out_weight, out_bias,
    up_weight, up_bias, down_weight, down_bias,
):
    vmem = pl.BlockSpec(memory_space=pltpu.VMEM)
    shape = jax.ShapeDtypeStruct
    row = shape((1, 16), F32)
    operands = (
        tokens, positions.reshape(1, 128), cotangent, ln1_gain, ln1_bias, ln2_gain, ln2_bias, qkv_weight[0],
        qkv_bias[0].transpose(0, 2, 1), out_weight[0].T, out_bias, up_weight[0], up_bias[0].T, down_weight[0].T,
        down_bias,
    )
    outs = (
        shape((128, 512), BF16), shape((128, 512), F32), row, row, row, row, shape((3, 16, 256), F32),
        shape((3, 2, 4), F32), shape((16, 256), F32), row, shape((16, 1024), F32), shape((2, 16), F32),
        shape((16, 1024), F32),
    )
    scratch = [
        ((4, 4, 2, 16, 768), BF16), ((16, 768), BF16), ((4, 4, 16, 128), BF16), ((3, 16, 128), BF16),
        ((2, 2, 128, 512), BF16), ((2, 2, 128, 512), BF16), ((2, 2, 1, 128), jnp.int32), ((16, 128), F32),
        ((2, 256, 512), F32), ((2, 256, 128), F32), ((2, 256, 512), BF16), ((2, 256, 512), BF16),
        ((512, 512), BF16), ((512, 512), BF16), ((512, 512), BF16),
        ((2, 256, 128), F32), ((2, 256, 128), F32), ((2, 256, 128), F32),
        ((512, 768), BF16), ((512, 128), BF16), ((512, 128), BF16),
        ((2, 2, 128, 512), BF16), ((2, 128, 512), BF16), ((2, 128, 512), BF16), ((3, 128, 512), BF16),
        ((2, 2, 128, 512), BF16), ((2, 128, 512), BF16), ((2, 128, 512), BF16), ((3, 128, 512), BF16),
        ((4, 4, 32, 768), BF16), ((3, 4, 32, 384), BF16), ((3, 4, 32, 384), BF16), ((4, 32, 384), BF16),
        ((4, 32, 384), BF16), ((3, 32, 384), BF16), ((3, 32, 384), BF16),
        ((4, 16, 128), BF16), ((3, 4, 16, 128), BF16), ((4, 16, 128), BF16), ((3, 16, 128), BF16),
        ((2, 16, 768), BF16), ((2, 2, 16, 768), BF16), ((16, 128), BF16), ((2, 2, 2, 16, 128), BF16),
    ]
    results = pl.pallas_call(
        kernel,
        out_shape=outs,
        in_specs=[vmem] * len(operands),
        out_specs=[vmem] * len(outs),
        scratch_shapes=[pltpu.VMEM(*item) for item in scratch]
        + [pltpu.SemaphoreType.DMA((M_ALL,)), pltpu.SemaphoreType.DMA((M_ALL,))],
        compiler_params=pltpu.CompilerParams(
            collective_id=0, has_side_effects=True, vmem_limit_bytes=48 * 1024 * 1024
        ),
    )(*operands)
    (
        output, grad_input, grad_gain1, grad_shift1, grad_gain2, grad_shift2, grad_qkv, grad_qkv_bias, grad_out,
        grad_bias, grad_up, grad_up_bias, grad_down,
    ) = results
    return (
        output, grad_input, grad_gain1, grad_shift1, grad_gain2, grad_shift2, grad_qkv[None],
        grad_qkv_bias.transpose(0, 2, 1)[None], grad_out.T[None], grad_bias, grad_up[None], grad_up_bias.T[None],
        grad_down.T[None], grad_bias,
    )


def solution(mesh):
    row = P(None, "fsdp")
    tokens = P(("fsdp", "ctx"), None)
    qkv, qkv_bias = P(None, None, "fsdp", "tp"), P(None, None, "tp", "fsdp")
    fanned, spread = P(None, "tp", "fsdp"), P(None, "fsdp", "tp")
    in_specs = (
        tokens, P(("fsdp", "ctx")), tokens, row, row, row, row, qkv, qkv_bias, fanned, row, spread, fanned, fanned, row
    )
    out_specs = (
        tokens, tokens, row, row, row, row, qkv, qkv_bias, fanned, row, spread, fanned, fanned, row
    )
    return jax.shard_map(body, mesh=mesh, in_specs=in_specs, out_specs=out_specs, check_vma=False)
```

time: 1520 us -> 59.1 us (0.04)
  waiting for transfers between devices: 831 us -> 0 us
  blocking collectives: 614 us -> 0 us
  Pallas kernels: 0 us -> 44.5 us
  other arithmetic: 20.1 us -> 0 us
  between operations: 17.7 us -> 0.75 us
  matrix products: 15.5 us -> 0 us
    all_gather x6 -> x0, blocking collectives: 370 us -> none  [the longest x1 83.6 us: gather_layer(): lax.all_gather(parts[4], 'fsdp', axis=1, tiled=True)]
    reduce_scatter x4 -> x0, waiting for transfers between devices: 362 us -> none  [the longest x1 183 us: reduce_terms(): lax.psum_scatter(terms[10].astype(jnp.bfloat16), 'fsdp', scatter_dimensio...]
    unnamed x12 -> x0, waiting for transfers between devices: 322 us -> none
    unnamed x2 -> x0, blocking collectives: 244 us -> none
    psum x2 -> x0, waiting for transfers between devices: 99.7 us -> none  [the longest x1 56.8 us: forward_layer(): lax.psum(partial_value.astype(jnp.bfloat16), 'tp').astype(jnp.float32)]
    all_gather x2 -> x0, waiting for transfers between devices: 46.4 us -> none  [the longest x1 46.4 us: gather_layer(): lax.all_gather(parts[10], 'fsdp', axis=1, tiled=True)]
    pallas_call x0 -> x1, Pallas kernels: none -> 44.5 us  [body(): pl.pallas_call(kernel, out_shape=outs, in_specs=[vmem] * len(operands), o...]
    dot_general x18 -> x0, matrix products: 15.5 us -> none  [the longest x1 2.62 us: forward_layer(): jnp.dot(mlp_input, w_up, preferred_element_type=jnp.float32)]
  transfers between devices with their start and end apart: 10 -> 0, of which waited for: 6 -> 0; matrix products, arithmetic and copies ran while one was open for 2% -> 0% of each run, Pallas kernels for 0% -> 0%
where the time goes in v1:
time: 59.1 us; the launch traced here: 58.8 us
  Pallas kernels  44.5 us (75%)
  local copies, waits for them, and re-layouts  13.5 us (23%)
  between operations  0.75 us (1%)
    pallas_call x1, Pallas kernels, body(): pl.pallas_call(kernel, out_shape=outs, in_specs=[vmem] * len(operands), o...  44.5 us
    unnamed x44, local copies, waits for them, and re-layouts  13.5 us

profile of v1, /device:TPU:1, one launch (start us, length us, event | category | flops | bytes accessed | tf_op | source)
XLA Modules:
  0.0 58.8 jit_solution(5034920495014807135)
XLA Ops:
  0.7 0.0 copy-start.5
  0.7 0.0 copy-start.11
  0.7 0.0 copy-start.12
  0.7 0.0 copy-start.13
  0.7 0.0 copy-start.6
  0.7 0.0 copy-start.10
  0.7 0.0 copy-start.7
  0.7 0.0 copy-start.8
  0.7 0.0 copy-start.9
  0.7 0.6 %copy-done.5 = bf16[1,256,16]{1,2,0:T(8,128)(2,1)S(1)} copy-done((bf16[1,256,16]{1,2,0:T(8,128)(2,1)S(1)}, bf16[1,256,16]{1,2,0:T(8,128)(2,1)}, u32[]{:S(2)}) %copy-start.5) | copy-done | bytes 8216
  1.3 0.0 copy-done.11
  1.4 0.0 copy-done.12
  1.4 0.0 copy-done.13
  1.4 0.0 copy-done.6
  1.4 0.0 copy-done.10
  1.4 0.0 copy-done.7
  1.4 0.0 copy-done.8
  1.4 0.0 copy-done.9
  1.4 0.0 copy-start
  1.4 0.9 %copy-done = bf16[128,512]{1,0:T(8,128)(2,1)S(1)} copy-done((bf16[128,512]{1,0:T(8,128)(2,1)S(1)}, bf16[128,512]{1,0:T(8,128)(2,1)}, u32[]{:S(2)}) %copy-start) | copy-done | bytes 131096
  2.3 0.0 copy-start.1
  2.3 0.9 %copy-done.1 = bf16[128,512]{1,0:T(8,128)(2,1)S(1)} copy-done((bf16[128,512]{1,0:T(8,128)(2,1)S(1)}, bf16[128,512]{1,0:T(8,128)(2,1)}, u32[]{:S(2)}) %copy-start.1) | copy-done | bytes 131096
  3.2 0.0 copy-start.2
  3.2 0.8 %copy-done.2 = bf16[1,16,1024]{2,1,0:T(8,128)(2,1)S(1)} copy-done((bf16[1,16,1024]{2,1,0:T(8,128)(2,1)S(1)}, bf16[1,16,1024]{2,1,0:T(8,128)(2,1)}, u32[]{:S(2)}) %copy-start.2) | copy-done | bytes 32792
  4.0 0.0 copy-start.3
  4.0 0.8 %copy-done.3 = bf16[1,1024,16]{1,2,0:T(8,128)(2,1)S(1)} copy-done((bf16[1,1024,16]{1,2,0:T(8,128)(2,1)S(1)}, bf16[1,1024,16]{1,2,0:T(8,128)(2,1)}, u32[]{:S(2)}) %copy-start.3) | copy-done | bytes 32792
  4.8 0.0 copy-start.4
  4.8 0.7 %copy-done.4 = bf16[1,3,16,256]{3,2,1,0:T(8,128)(2,1)S(1)} copy-done((bf16[1,3,16,256]{3,2,1,0:T(8,128)(2,1)S(1)}, bf16[1,3,16,256]{3,2,1,0:T(8,128)(2,1)}, u32[]{:S(2)}) %copy-start.4) | copy-done | bytes 24600
  5.5 0.0 copy-start.14
  5.5 0.7 %copy-done.14 = bf16[1,16]{1,0:T(2,128)(2,1)S(1)} copy-done((bf16[1,16]{1,0:T(2,128)(2,1)S(1)}, bf16[1,16]{1,0:T(2,128)(2,1)}, u32[]{:S(2)}) %copy-start.14) | copy-done | bytes 56
  6.2 44.5 %shard_map.254 = (bf16[128,512]{1,0:T(8,128)(2,1)S(1)}, f32[128,512]{1,0:T(8,128)S(1)}, f32[1,16]{1,0:T(1,128)S(1)}, f32[1,16]{1,0:T(1,128)S(1)}, f32[1,16]{1,0:...) custom-call(bf16[128,512]{1,0:T(8,128)(2,1)S(1)} %copy-done, ...), custom_call_target="tpu_custom_call" | custom-call | tf_op jit(solution)/shard_map/pallas_call | solution.py:515
  50.7 0.5 copy.43
  51.2 0.7 %copy.44 = bf16[128,512]{1,0:T(8,128)(2,1)} copy(bf16[128,512]{1,0:T(8,128)(2,1)S(1)} %get-tuple-element.82) | data formatting | bytes 262144
  51.9 0.7 %copy.45 = f32[128,512]{1,0:T(8,128)} copy(f32[128,512]{1,0:T(8,128)S(1)} %get-tuple-element.83) | data formatting | bytes 524288
  52.6 0.5 copy.46
  53.1 0.5 copy.47
  53.6 0.5 copy.48
  54.1 0.5 copy.49
  54.6 0.6 %copy.50 = f32[1,3,16,256]{3,2,1,0:T(8,128)} copy(f32[1,3,16,256]{3,2,1,0:T(8,128)S(1)} %bitcast.31) | data formatting | bytes 98304
  55.2 0.6 copy.51
  55.8 0.6 %copy.52 = f32[1,256,16]{1,2,0:T(8,128)} copy(f32[1,256,16]{1,2,0:T(8,128)S(1)} %bitcast.35) | data formatting | bytes 32768
  56.4 0.5 copy.53
  56.9 0.6 %copy.54 = f32[1,16,1024]{2,1,0:T(8,128)} copy(f32[1,16,1024]{2,1,0:T(8,128)S(1)} %bitcast.30) | data formatting | bytes 131072
  57.6 0.6 copy.55
  58.1 0.6 %copy.56 = f32[1,1024,16]{1,2,0:T(8,128)} copy(f32[1,1024,16]{1,2,0:T(8,128)S(1)} %bitcast.29) | data formatting | bytes 131072
Async XLA Ops:
  0.7 0.7 %copy-start.5 = (bf16[1,256,16]{1,2,0:T(8,128)(2,1)S(1)}, bf16[1,256,16]{1,2,0:T(8,128)(2,1)}, u32[]{:S(2)}) copy-start(bf16[1,256,16]{1,2,0:T(8,128)(2,1)} %param.24) | copy-start | bytes 24580
  0.7 0.7 %copy-start.11 = (bf16[1,16]{1,0:T(2,128)(2,1)S(1)}, bf16[1,16]{1,0:T(2,128)(2,1)}, u32[]{:S(2)}) copy-start(bf16[1,16]{1,0:T(2,128)(2,1)} %shift2.1) | copy-start | bytes 100
  0.7 0.7 %copy-start.12 = (bf16[1,16]{1,0:T(2,128)(2,1)S(1)}, bf16[1,16]{1,0:T(2,128)(2,1)}, u32[]{:S(2)}) copy-start(bf16[1,16]{1,0:T(2,128)(2,1)} %out_b.1) | copy-start | bytes 100
  0.7 0.7 %copy-start.13 = (bf16[1,16,2]{1,2,0:T(2,128)(2,1)S(1)}, bf16[1,16,2]{1,2,0:T(2,128)(2,1)}, u32[]{:S(2)}) copy-start(bf16[1,16,2]{1,2,0:T(2,128)(2,1)} %param.27) | copy-start | bytes 196
  0.7 0.7 %copy-start.6 = (bf16[1,3,4,2]{2,3,1,0:T(2,128)(2,1)S(1)}, bf16[1,3,4,2]{2,3,1,0:T(2,128)(2,1)}, u32[]{:S(2)}) copy-start(bf16[1,3,4,2]{2,3,1,0:T(2,128)(2,1)} %param.23) | copy-start | bytes 148
  0.7 0.7 %copy-start.10 = (bf16[1,16]{1,0:T(2,128)(2,1)S(1)}, bf16[1,16]{1,0:T(2,128)(2,1)}, u32[]{:S(2)}) copy-start(bf16[1,16]{1,0:T(2,128)(2,1)} %gain2.1) | copy-start | bytes 100
  0.7 0.7 %copy-start.7 = (s32[128]{0:T(128)S(1)}, s32[128]{0:T(128)}, u32[]{:S(2)}) copy-start(s32[128]{0:T(128)} %param.16) | copy-start | bytes 1540
  0.7 0.7 %copy-start.8 = (bf16[1,16]{1,0:T(2,128)(2,1)S(1)}, bf16[1,16]{1,0:T(2,128)(2,1)}, u32[]{:S(2)}) copy-start(bf16[1,16]{1,0:T(2,128)(2,1)} %gain1.1) | copy-start | bytes 100
  0.7 0.7 %copy-start.9 = (bf16[1,16]{1,0:T(2,128)(2,1)S(1)}, bf16[1,16]{1,0:T(2,128)(2,1)}, u32[]{:S(2)}) copy-start(bf16[1,16]{1,0:T(2,128)(2,1)} %shift1.1) | copy-start | bytes 100
  1.4 0.9 %copy-start = (bf16[128,512]{1,0:T(8,128)(2,1)S(1)}, bf16[128,512]{1,0:T(8,128)(2,1)}, u32[]{:S(2)}) copy-start(bf16[128,512]{1,0:T(8,128)(2,1)} %tok_in.1) | copy-start | bytes 393220
  2.3 0.9 %copy-start.1 = (bf16[128,512]{1,0:T(8,128)(2,1)S(1)}, bf16[128,512]{1,0:T(8,128)(2,1)}, u32[]{:S(2)}) copy-start(bf16[128,512]{1,0:T(8,128)(2,1)} %cot_in.1) | copy-start | bytes 393220
  3.2 0.8 %copy-start.2 = (bf16[1,16,1024]{2,1,0:T(8,128)(2,1)S(1)}, bf16[1,16,1024]{2,1,0:T(8,128)(2,1)}, u32[]{:S(2)}) copy-start(bf16[1,16,1024]{2,1,0:T(8,128)(2,1)} %param.26) | copy-start | bytes 98308
  4.0 0.8 %copy-start.3 = (bf16[1,1024,16]{1,2,0:T(8,128)(2,1)S(1)}, bf16[1,1024,16]{1,2,0:T(8,128)(2,1)}, u32[]{:S(2)}) copy-start(bf16[1,1024,16]{1,2,0:T(8,128)(2,1)} %param.28) | copy-start | bytes 98308
  4.8 0.7 %copy-start.4 = (bf16[1,3,16,256]{3,2,1,0:T(8,128)(2,1)S(1)}, bf16[1,3,16,256]{3,2,1,0:T(8,128)(2,1)}, u32[]{:S(2)}) copy-start(bf16[1,3,16,256]{3,2,1,0:T(8,128)(2,1)} %param.22) | copy-start | bytes 73732
  5.5 0.7 %copy-start.14 = (bf16[1,16]{1,0:T(2,128)(2,1)S(1)}, bf16[1,16]{1,0:T(2,128)(2,1)}, u32[]{:S(2)}) copy-start(bf16[1,16]{1,0:T(2,128)(2,1)} %down_b.1) | copy-start | bytes 100

commit v2 on v1

--- a/solution.py
+++ b/solution.py
@@ -19,6 +19,7 @@
 MESH = pl.DeviceIdType.MESH
 F32 = jnp.float32
 BF16 = jnp.bfloat16
+GRANT = int(62 * 1024 * 1024)
 
 UP = slice(0, 256)
 QK = slice(256, 384)
@@ -69,13 +70,15 @@
 
 
 def kernel(
-    tok_in, pos_in, cot_in, gain1, shift1, gain2, shift2, qkv_w, qkv_b, out_w, out_b, up_w, up_b, down_w, down_b,
+    tok_in, pos_in, cot_in, gain1_in, shift1_in, gain2_in, shift2_in, qkv_w_in, qkv_b_in, out_w_in, out_b_in, up_w_in,
+    up_b_in, down_w_in, down_b_in,
     out_o, gin_o, gg1_o, gb1_o, gg2_o, gb2_o, gqkvw_o, gqkvb_o, goutw_o, gbias_o, gupw_o, gupb_o, gdownw_o,
+    gain1, shift1, gain2, shift2, qkv_w, qkv_b, out_w, out_b, up_w, up_b, down_w, down_b,
     W, XS, E, XE, TK, CT, PS, SM,
     NRM, RSQ, NB, MB, NTR, MTR, BTR, COS, SIN, PCOL,
     GC, GVZ, ATZ, PO, RO, SO, XO, PD, RD, SD, XD,
     GS, RA1, RB1, SA, SB, RA2, RB2, EG, RE1, SE, RE2, FB, XR, FE, XF,
-    ss, rs,
+    ss, rs, ls,
 ):
     place = lax.axis_index("fsdp")
     z, y, xh = place // 8, (place // 2) % 4, place % 2
@@ -114,6 +117,17 @@
     for peer in peers:
         pl.semaphore_signal(barrier, inc=1, device_id=peer, device_id_type=MESH)
 
+    loads = []
+    for i, (src, dst) in enumerate((
+        (qkv_w_in, qkv_w), (out_w_in, out_w), (up_w_in, up_w), (down_w_in, down_w), (gain1_in, gain1),
+        (shift1_in, shift1), (gain2_in, gain2), (shift2_in, shift2), (out_b_in, out_b), (down_b_in, down_b),
+        (qkv_b_in, qkv_b), (up_b_in, up_b), (pos_in, PS.at[xh, c]), (tok_in, TK.at[xh, c]), (cot_in, CT.at[xh, c]),
+    )):
+        loads.append(pltpu.make_async_copy(src, dst, ls.at[i]))
+        loads[-1].start()
+    for load in loads[:4]:
+        load.wait()
+
     def cut(xx):
         lanes = pl.ds(pl.multiple_of(xx * 128, 128), 128)
         q_pair, k_pair, v_pair, o_pair = (
@@ -137,6 +151,8 @@
         target[:, DN] = down_cut
         target[:, VO] = vo_cut
 
+    for load in loads[4:12]:
+        load.wait()
     SM[...] = jnp.zeros((16, 128), F32)
     for row, ref in enumerate((gain1, shift1, gain2, shift2, out_b, down_b)):
         SM[row : row + 1, 0:16] = ref[...].astype(F32)
@@ -165,10 +181,6 @@
 
     XE[0] = placed(ox).astype(BF16)
     XE[1] = placed(xh).astype(BF16)
-
-    TK[xh, c] = tok_in[...]
-    CT[xh, c] = cot_in[...]
-    PS[xh, c] = pos_in[...]
 
     pl.semaphore_wait(barrier, len(peers))
 
@@ -211,6 +223,8 @@
         ag2.append(track(send(M_AG2 + 3 + k - 1, here, here, zdev(k))))
     cot_across.wait_recv()
     cot_pass = track(send(M_COT + 2, CT.at[ox, c], CT.at[ox, c], core))
+    for load in loads[12:]:
+        load.wait()
     tok_core.wait_recv()
     tok_pass.wait_recv()
 
@@ -403,10 +417,10 @@
 
     for copy in out_copies:
         copy.wait_recv()
-    out_o[...] = (tok_in[...].astype(F32) + (over_chips(SO[xh], XO) + b_branch)).astype(BF16)
+    out_o[...] = (TK[xh, c].astype(F32) + (over_chips(SO[xh], XO) + b_branch)).astype(BF16)
     for copy in dx_copies:
         copy.wait_recv()
-    gin_o[...] = cot_in[...].astype(F32) + over_chips(SD[xh], XD)
+    gin_o[...] = CT[xh, c].astype(F32) + over_chips(SD[xh], XD)
 
     for copy in rs2:
         copy.wait_recv()
@@ -476,16 +490,23 @@
     for which in range(3):
         gqkvb_o[which] = new_qkv[which]
     gupb_o[...] = new_up
-
     for copy in sent:
         copy.wait_send()
+
+
+def place_results(*refs):
+    ins, outs, sems = refs[:13], refs[13:27], refs[27]
+    copies = [pltpu.make_async_copy(src, dst, sems.at[i]) for i, (src, dst) in enumerate(zip(ins + (ins[9],), outs))]
+    for copy in copies:
+        copy.start()
+    for copy in copies:
+        copy.wait()
 
 
 def body(
     tokens, positions, cotangent, ln1_gain, ln1_bias, ln2_gain, ln2_bias, qkv_weight, qkv_bias, out_weight, out_bias,
     up_weight, up_bias, down_weight, down_bias,
 ):
-    vmem = pl.BlockSpec(memory_space=pltpu.VMEM)
     shape = jax.ShapeDtypeStruct
     row = shape((1, 16), F32)
     operands = (
@@ -499,6 +520,8 @@
         shape((16, 1024), F32),
     )
     scratch = [
+        *[((1, 16), BF16)] * 4, ((3, 16, 256), BF16), ((3, 2, 4), BF16), ((16, 256), BF16), ((1, 16), BF16),
+        ((16, 1024), BF16), ((2, 16), BF16), ((16, 1024), BF16), ((1, 16), BF16),
         ((4, 4, 2, 16, 768), BF16), ((16, 768), BF16), ((4, 4, 16, 128), BF16), ((3, 16, 128), BF16),
         ((2, 2, 128, 512), BF16), ((2, 2, 128, 512), BF16), ((2, 2, 1, 128), jnp.int32), ((16, 128), F32),
         ((2, 256, 512), F32), ((2, 256, 128), F32), ((2, 256, 512), BF16), ((2, 256, 512), BF16),
@@ -515,22 +538,30 @@
     results = pl.pallas_call(
         kernel,
         out_shape=outs,
-        in_specs=[vmem] * len(operands),
-        out_specs=[vmem] * len(outs),
+        in_specs=[pl.BlockSpec(memory_space=pl.ANY)] * len(operands),
+        out_specs=[pl.BlockSpec(memory_space=pltpu.VMEM)] * len(outs),
         scratch_shapes=[pltpu.VMEM(*item) for item in scratch]
-        + [pltpu.SemaphoreType.DMA((M_ALL,)), pltpu.SemaphoreType.DMA((M_ALL,))],
+        + [pltpu.SemaphoreType.DMA((M_ALL,)), pltpu.SemaphoreType.DMA((M_ALL,)), pltpu.SemaphoreType.DMA((15,))],
         compiler_params=pltpu.CompilerParams(
-            collective_id=0, has_side_effects=True, vmem_limit_bytes=48 * 1024 * 1024
+            collective_id=0, has_side_effects=True, vmem_limit_bytes=GRANT
         ),
     )(*operands)
+    results = pl.pallas_call(
+        place_results,
+        out_shape=outs + (row,),
+        in_specs=[pl.BlockSpec(memory_space=pltpu.VMEM)] * 13,
+        out_specs=[pl.BlockSpec(memory_space=pl.ANY)] * 14,
+        scratch_shapes=[pltpu.SemaphoreType.DMA((14,))],
+        compiler_params=pltpu.CompilerParams(vmem_limit_bytes=GRANT),
+    )(*results)
     (
         output, grad_input, grad_gain1, grad_shift1, grad_gain2, grad_shift2, grad_qkv, grad_qkv_bias, grad_out,
-        grad_bias, grad_up, grad_up_bias, grad_down,
+        grad_bias, grad_up, grad_up_bias, grad_down, grad_bias_again,
     ) = results
     return (
         output, grad_input, grad_gain1, grad_shift1, grad_gain2, grad_shift2, grad_qkv[None],
         grad_qkv_bias.transpose(0, 2, 1)[None], grad_out.T[None], grad_bias, grad_up[None], grad_up_bias.T[None],
-        grad_down.T[None], grad_bias,
+        grad_down.T[None], grad_bias_again,
     )
 
 

time: 59.1 us -> 48.4 us (0.82)
  local copies, waits for them, and re-layouts: 13.5 us -> 0 us
  Pallas kernels: 44.5 us -> 47.6 us
    unnamed x44 -> x0, local copies, waits for them, and re-layouts: 13.5 us -> none
    pallas_call x1 -> x2, Pallas kernels: 44.5 us -> 47.6 us  [the longest x1 45.6 us: body(): pl.pallas_call(kernel, out_shape=outs, in_specs=[pl.BlockSpec(memory_spac...]
where the time goes in v2:
time: 48.4 us; the launch traced here: 48.2 us
  Pallas kernels  47.6 us (98%)
  between operations  0.66 us (1%)
    pallas_call x1, Pallas kernels, body(): pl.pallas_call(kernel, out_shape=outs, in_specs=[pl.BlockSpec(memory_spac...  45.6 us
    pallas_call x1, Pallas kernels, body(): pl.pallas_call(place_results, out_shape=outs + (row,), in_specs=[pl.Block...  2.02 us

profile of v2, /device:TPU:1, one launch (start us, length us, event | category | flops | bytes accessed | tf_op | source)
XLA Modules:
  0.0 48.2 jit_solution(17941531288828126828)
XLA Ops:
  0.7 45.6 %shard_map.254 = (bf16[128,512]{1,0:T(8,128)(2,1)}, f32[128,512]{1,0:T(8,128)}, f32[1,16]{1,0:T(1,128)}, f32[1,16]{1,0:T(1,128)}, f32[1,16]{1,0:T(1,128)}, /*ind...) custom-call(bf16[128,512]{1,0:T(8,128)(2,1)} %tok_in.1, ...), custom_call_target="tpu_custom_call" | custom-call | tf_op jit(solution)/shard_map/pallas_call | solution.py:538
  46.2 2.0 %shard_map.255 = (bf16[128,512]{1,0:T(8,128)(2,1)}, f32[128,512]{1,0:T(8,128)}, f32[1,16]{1,0:T(1,128)}, f32[1,16]{1,0:T(1,128)}, f32[1,16]{1,0:T(1,128)}, /*ind...) custom-call(bf16[128,512]{1,0:T(8,128)(2,1)} %get-tuple-element.41.r, ...), custom_call_target="tpu_custom_call" | custom-call | tf_op jit(solution)/shard_map/pallas_call | solution.py:549

commit v3 on v2

--- a/solution.py
+++ b/solution.py
@@ -27,6 +27,8 @@
 VO = slice(640, 768)
 HALF = (slice(0, 384), slice(384, 768))
 
+PARTS = ((0, UP), (1, DN), (0, QK), (1, VO))
+
 M_XW, M_XE = 0, 1
 M_POS = 2
 M_TOK = 5
@@ -34,16 +36,16 @@
 M_AG1 = 12
 M_AGE1 = 18
 M_AG2 = 21
-M_AGE2 = 27
-M_OUT = 30
-M_DX = 34
-M_RS1 = 38
-M_RSE1 = 44
-M_RS2 = 47
-M_RSE2 = 53
-M_FIN = 56
-M_FINE = 59
-M_ALL = 66
+M_AGE2 = 33
+M_OUT = 36
+M_DX = 40
+M_RS1 = 46
+M_RSE1 = 58
+M_RS2 = 61
+M_RSE2 = 73
+M_FIN = 76
+M_FINE = 79
+M_ALL = 86
 
 
 def dot_nn(left, right):
@@ -76,7 +78,7 @@
     gain1, shift1, gain2, shift2, qkv_w, qkv_b, out_w, out_b, up_w, up_b, down_w, down_b,
     W, XS, E, XE, TK, CT, PS, SM,
     NRM, RSQ, NB, MB, NTR, MTR, BTR, COS, SIN, PCOL,
-    GC, GVZ, ATZ, PO, RO, SO, XO, PD, RD, SD, XD,
+    GC, GVZ, ATZ, PO, RO, SO, XO, TO, PD, RD, SD, XD, TD,
     GS, RA1, RB1, SA, SB, RA2, RB2, EG, RE1, SE, RE2, FB, XR, FE, XF,
     ss, rs, ls,
 ):
@@ -216,11 +218,11 @@
     age2 = []
     for k in (2, 1, 3):
         age2.append(track(send(M_AGE2 + k - 1, E.at[:, y], E.at[:, y], ydev(k))))
-    for k in (2, 1, 3):
-        here = W.at[:, y, :, :, HALF[0]]
-        ag2.append(track(send(M_AG2 + k - 1, here, here, ydev(k))))
-        here = W.at[z, :, :, :, HALF[1]]
-        ag2.append(track(send(M_AG2 + 3 + k - 1, here, here, zdev(k))))
+    for part, (route, columns) in enumerate(PARTS):
+        for k in (2, 1, 3):
+            here = (W.at[:, y, :, :, columns], W.at[z, :, :, :, columns])[route]
+            number = M_AG2 + 3 * part + k - 1
+            ag2.append(track(send(number, here, here, (ydev, zdev)[route](k))))
     cot_across.wait_recv()
     cot_pass = track(send(M_COT + 2, CT.at[ox, c], CT.at[ox, c], core))
     for load in loads[12:]:
@@ -286,30 +288,52 @@
         NTR[:, s * 256 : (s + 1) * 256] = normed.T
         MTR[:, s * 256 : (s + 1) * 256] = mlp_input.T
 
-    for copy in ag2:
-        copy.wait_recv()
+    for copy in ag2[:6]:
+        copy.wait_recv()
+
+    def columns_of(columns, width):
+        return W[:, :, :, :, columns].reshape(512, width)
 
     gb_up = jnp.zeros((1, 256), F32)
+    for s in range(2):
+        part = slice(s * 256, (s + 1) * 256)
+        branch_grad = CT[s].reshape(256, 512)
+        pre_act = dot_nn(MB[s], columns_of(UP, 256)) + b_up
+        phi = 0.5 * (1.0 + lax.erf(pre_act * INV_ROOT_TWO))
+        density = jnp.exp(-0.5 * pre_act * pre_act) * INV_ROOT_TWO_PI
+        grad_hidden = dot_nn(branch_grad, columns_of(DN, 256))
+        grad_pre = (grad_hidden * (phi + pre_act * density)).astype(BF16)
+        gb_up = gb_up + jnp.sum(grad_pre.astype(F32), axis=0, keepdims=True)
+        GC[part, UP] = grad_pre
+        GC[part, DN] = (pre_act * phi).astype(BF16)
+
+    rs1 = []
+
+    def first_ring(part):
+        route, columns = PARTS[part]
+        for k in (2, 1, 3):
+            src = (GS.at[:, (y + k) % 4, :, columns], GS.at[(z + k) % 4, :, :, columns])[route]
+            dst = (RA1, RB1)[route].at[k - 1, :, :, local(columns)]
+            rs1.append(track(send(M_RS1 + 3 * part + k - 1, src, dst, (ydev, zdev)[route](k))))
+
+    def local(columns):
+        return slice(columns.start % 384, (columns.stop - 1) % 384 + 1)
+
+    GS[:, :, :, UP] = dot_nn(MTR[...], GC[:, UP]).astype(BF16).reshape(4, 4, 32, 256)
+    first_ring(0)
+    GS[:, :, :, DN] = dot_nn(BTR[...], GC[:, DN]).astype(BF16).reshape(4, 4, 32, 256)
+    first_ring(1)
+
+    for copy in ag2[6:]:
+        copy.wait_recv()
     gb_qk = jnp.zeros((1, 128), F32)
     gb_v = jnp.zeros((1, HD), F32)
     for s in range(2):
         part = slice(s * 256, (s + 1) * 256)
-        normed, mlp_input, branch_grad = NB[s], MB[s], CT[s].reshape(256, 512)
-        w_up = W[:, :, :, :, UP].reshape(512, 256)
-        w_down = W[:, :, :, :, DN].reshape(512, 256)
-        w_qk = W[:, :, :, :, QK].reshape(512, 128)
-        w_vo = W[:, :, :, :, VO].reshape(512, 128)
-        pre_act = dot_nn(mlp_input, w_up) + b_up
-        phi = 0.5 * (1.0 + lax.erf(pre_act * INV_ROOT_TWO))
-        density = jnp.exp(-0.5 * pre_act * pre_act) * INV_ROOT_TWO_PI
-        activated = (pre_act * phi).astype(BF16)
-        grad_pre = (dot_nn(branch_grad, w_down) * (phi + pre_act * density)).astype(BF16)
-        gb_up = gb_up + jnp.sum(grad_pre.astype(F32), axis=0, keepdims=True)
-        GC[part, UP] = grad_pre
-        GC[part, DN] = activated
-
+        normed, branch_grad = NB[s], CT[s].reshape(256, 512)
+        w_vo = columns_of(VO, 128)
         cos, sin = COS[s], SIN[s]
-        qk = dot_nn(normed, w_qk) + b_qk
+        qk = dot_nn(normed, columns_of(QK, 128)) + b_qk
         qk = (qk * cos + turn_partner(qk) * sin).astype(BF16)
         query, key = qk[:, :HD], qk[:, HD:]
         value = (dot_nn(normed, w_vo)[:, :HD] + b_v).astype(BF16)
@@ -336,47 +360,45 @@
         GC[part, QK] = grad_qk
         GVZ[part] = jnp.concatenate([grad_value, blank], axis=1)
         ATZ[part] = jnp.concatenate([blank, attended], axis=1)
-        branch = dot_nt(activated, w_down) + dot_nt(ATZ[part], w_vo)
+
+    def rows_of(s):
+        return pl.ds(pl.multiple_of(s * 256, 256), 256)
+
+    out_core = []
+    for i, s in enumerate((ox, xh)):
+        part = rows_of(s)
+        branch = dot_nt(GC[part, DN], columns_of(DN, 256)) + dot_nt(ATZ[part], columns_of(VO, 128))
         PO[s] = branch.astype(BF16).reshape(2, 128, 512)
-
-    out_core = track(send(M_OUT, PO.at[:, oc], RO, core))
-
-    GS[:, :, :, UP] = dot_nn(MTR[...], GC[:, UP]).astype(BF16).reshape(4, 4, 32, 256)
+        out_core.append(track(send(M_OUT + i, PO.at[s, oc], RO.at[s], core)))
+
     GS[:, :, :, QK] = dot_nn(NTR[...], GC[:, QK]).astype(BF16).reshape(4, 4, 32, 128)
-    rs1 = []
-    for k in (2, 1, 3):
-        rs1.append(track(send(M_RS1 + k - 1, GS.at[:, (y + k) % 4, :, HALF[0]], RA1.at[k - 1], ydev(k))))
-    GS[:, :, :, DN] = dot_nn(BTR[...], GC[:, DN]).astype(BF16).reshape(4, 4, 32, 256)
+    first_ring(2)
     grad_vo = dot_nn(NTR[...], GVZ[...]) + dot_nn(BTR[...], ATZ[...])
     GS[:, :, :, VO] = grad_vo.astype(BF16).reshape(4, 4, 32, 128)
-    for k in (2, 1, 3):
-        rs1.append(track(send(M_RS1 + 3 + k - 1, GS.at[(z + k) % 4, :, :, HALF[1]], RB1.at[k - 1], zdev(k))))
-
-    out_core.wait_recv()
-    SO[...] = (PO[:, c].astype(F32) + RO[...].astype(F32)).astype(BF16)
-    out_copies = [
-        track(send(M_OUT + 1, SO.at[ox], XO.at[0], dev(ox, c, ot))),
-        track(send(M_OUT + 2, SO.at[ox], XO.at[1], dev(ox, c, t))),
-        track(send(M_OUT + 3, SO.at[xh], XO.at[2], dev(xh, c, ot))),
-    ]
+    first_ring(3)
+
+    def over_cores(s, own, received, total):
+        total[s] = (own[s, c].astype(F32) + received[s].astype(F32)).astype(BF16)
+
+    out_core[0].wait_recv()
+    over_cores(ox, PO, RO, SO)
+    out_across = track(send(M_OUT + 2, SO.at[ox], XO.at[0], dev(ox, c, ot)))
 
     totals = [jnp.zeros((1, 512), F32) for _ in range(4)]
-    for s in range(2):
-        part = slice(s * 256, (s + 1) * 256)
-        w_up = W[:, :, :, :, UP].reshape(512, 256)
-        w_qk = W[:, :, :, :, QK].reshape(512, 128)
-        w_vo = W[:, :, :, :, VO].reshape(512, 128)
+    dx_core = []
+    for i, s in enumerate((ox, xh)):
+        part = rows_of(s)
         n = NRM[s]
-        grad_mlp = dot_nt(GC[part, UP], w_up)
-        grad_normed = dot_nt(GC[part, QK], w_qk) + dot_nt(GVZ[part], w_vo)
-        for i, term in enumerate((grad_normed * n, grad_normed, grad_mlp * n, grad_mlp)):
-            totals[i] = totals[i] + jnp.sum(term, axis=0, keepdims=True)
+        grad_mlp = dot_nt(GC[part, UP], columns_of(UP, 256))
+        grad_normed = dot_nt(GC[part, QK], columns_of(QK, 128)) + dot_nt(GVZ[part], columns_of(VO, 128))
+        for j, term in enumerate((grad_normed * n, grad_normed, grad_mlp * n, grad_mlp)):
+            totals[j] = totals[j] + jnp.sum(term, axis=0, keepdims=True)
         joined = grad_normed * g1 + grad_mlp * g2
         mean_one = jnp.mean(joined, axis=1, keepdims=True)
         mean_two = jnp.mean(joined * n, axis=1, keepdims=True)
         term = RSQ[s][:, :1] * (joined - mean_one - n * mean_two)
         PD[s] = term.astype(BF16).reshape(2, 128, 512)
-    dx_core = track(send(M_DX, PD.at[:, oc], RD, core))
+        dx_core.append(track(send(M_DX + i, PD.at[s, oc], RD.at[s], core)))
 
     up_rows = jnp.concatenate([gb_up[:, :128], gb_up[:, 128:]], axis=0)
     v_row = jnp.concatenate([gb_v, jnp.zeros((1, 128 - HD), F32)], axis=1)
@@ -386,16 +408,17 @@
         EG[zz] = jnp.concatenate(pieces + [jnp.zeros((7, 128), F32)], axis=0).astype(BF16)
     rse1 = [track(send(M_RSE1 + k - 1, EG, RE1.at[k - 1], ydev(k))) for k in (2, 1, 3)]
 
-    dx_core.wait_recv()
-    SD[...] = (PD[:, c].astype(F32) + RD[...].astype(F32)).astype(BF16)
-    dx_copies = [
-        track(send(M_DX + 1, SD.at[ox], XD.at[0], dev(ox, c, ot))),
-        track(send(M_DX + 2, SD.at[ox], XD.at[1], dev(ox, c, t))),
-        track(send(M_DX + 3, SD.at[xh], XD.at[2], dev(xh, c, ot))),
+    dx_core[0].wait_recv()
+    over_cores(ox, PD, RD, SD)
+    parts_of_rows = (slice(0, 64), slice(64, 128))
+    dx_across = [
+        track(send(M_DX + 2 + i, SD.at[ox, part], XD.at[0, part], dev(ox, c, ot)))
+        for i, part in enumerate(parts_of_rows)
     ]
-
-    for copy in rs1:
-        copy.wait_recv()
+    dx_core[1].wait_recv()
+    over_cores(xh, PD, RD, SD)
+    out_core[1].wait_recv()
+    over_cores(xh, PO, RO, SO)
 
     def summed(own, received):
         total = own.astype(F32)
@@ -403,24 +426,40 @@
             total = total + received[k].astype(F32)
         return total
 
-    SA[...] = summed(GS[:, y, :, HALF[0]], RA1).astype(BF16)
-    rs2 = [track(send(M_RS2 + k - 1, SA.at[(z + k) % 4], RA2.at[k - 1], zdev(k))) for k in (2, 1, 3)]
-    SB[...] = summed(GS[z, :, :, HALF[1]], RB1).astype(BF16)
-    rs2 += [track(send(M_RS2 + 3 + k - 1, SB.at[(y + k) % 4], RB2.at[k - 1], ydev(k))) for k in (2, 1, 3)]
+    rs2 = []
+
+    def second_ring(part):
+        route, columns = PARTS[part]
+        for copy in rs1[3 * part : 3 * part + 3]:
+            copy.wait_recv()
+        here = local(columns)
+        if route == 0:
+            SA[:, :, here] = summed(GS[:, y, :, columns], RA1[:, :, :, here]).astype(BF16)
+        else:
+            SB[:, :, here] = summed(GS[z, :, :, columns], RB1[:, :, :, here]).astype(BF16)
+        for k in (2, 1, 3):
+            src = (SA.at[(z + k) % 4, :, here], SB.at[(y + k) % 4, :, here])[route]
+            dst = (RA2, RB2)[route].at[k - 1, :, here]
+            rs2.append(track(send(M_RS2 + 3 * part + k - 1, src, dst, (zdev, ydev)[route](k))))
+
+    second_ring(0)
+    second_ring(1)
+    out_across.wait_recv()
+    TO[...] = (SO[xh].astype(F32) + XO[0].astype(F32)).astype(BF16)
+    out_pair = track(send(M_OUT + 3, TO, XO.at[1], dev(xh, c, ot)))
+
+    second_ring(2)
+    second_ring(3)
+    dx_pair = []
+    for i, part in enumerate(parts_of_rows):
+        dx_across[i].wait_recv()
+        TD[part] = (SD[xh, part].astype(F32) + XD[0, part].astype(F32)).astype(BF16)
+        dx_pair.append(track(send(M_DX + 4 + i, TD.at[part], XD.at[1, part], dev(xh, c, ot))))
+
     for copy in rse1:
         copy.wait_recv()
     SE[...] = summed(EG[...], RE1).astype(BF16)
     rse2 = [track(send(M_RSE2 + k - 1, SE.at[(z + k) % 4], RE2.at[k - 1], zdev(k))) for k in (2, 1, 3)]
-
-    def over_chips(own, received):
-        return (own.astype(F32) + received[2].astype(F32)) + (received[0].astype(F32) + received[1].astype(F32))
-
-    for copy in out_copies:
-        copy.wait_recv()
-    out_o[...] = (TK[xh, c].astype(F32) + (over_chips(SO[xh], XO) + b_branch)).astype(BF16)
-    for copy in dx_copies:
-        copy.wait_recv()
-    gin_o[...] = CT[xh, c].astype(F32) + over_chips(SD[xh], XD)
 
     for copy in rs2:
         copy.wait_recv()
@@ -437,6 +476,14 @@
     FE[...] = summed(SE[z], RE2).astype(BF16)
     fine = [track(send(M_FINE + i, FE, XF.at[t, xh, c], where)) for i, where in enumerate(group)]
     XF[t, xh, c] = FE[...]
+
+    for copy in dx_pair:
+        copy.wait_recv()
+    gin_o[...] = CT[xh, c].astype(F32) + (TD[...].astype(F32) + XD[1].astype(F32))
+
+    out_pair.wait_recv()
+    total = TO[...].astype(F32) + XO[1].astype(F32)
+    out_o[...] = (TK[xh, c].astype(F32) + (total + b_branch)).astype(BF16)
 
     for copy in fin:
         copy.wait_recv()
@@ -528,8 +575,9 @@
         ((512, 512), BF16), ((512, 512), BF16), ((512, 512), BF16),
         ((2, 256, 128), F32), ((2, 256, 128), F32), ((2, 256, 128), F32),
         ((512, 768), BF16), ((512, 128), BF16), ((512, 128), BF16),
-        ((2, 2, 128, 512), BF16), ((2, 128, 512), BF16), ((2, 128, 512), BF16), ((3, 128, 512), BF16),
-        ((2, 2, 128, 512), BF16), ((2, 128, 512), BF16), ((2, 128, 512), BF16), ((3, 128, 512), BF16),
+        ((2, 2, 128, 512), BF16), ((2, 128, 512), BF16), ((2, 128, 512), BF16), ((2, 128, 512), BF16),
+        ((128, 512), BF16), ((2, 2, 128, 512), BF16), ((2, 128, 512), BF16), ((2, 128, 512), BF16),
+        ((2, 128, 512), BF16), ((128, 512), BF16),
         ((4, 4, 32, 768), BF16), ((3, 4, 32, 384), BF16), ((3, 4, 32, 384), BF16), ((4, 32, 384), BF16),
         ((4, 32, 384), BF16), ((3, 32, 384), BF16), ((3, 32, 384), BF16),
         ((4, 16, 128), BF16), ((3, 4, 16, 128), BF16), ((4, 16, 128), BF16), ((3, 16, 128), BF16),

time: 48.4 us -> 45.6 us (0.942)
  Pallas kernels: 47.6 us -> 44.7 us
    pallas_call x1, Pallas kernels: 45.6 us -> 42.7 us  [body(): pl.pallas_call(kernel, out_shape=outs, in_specs=[pl.BlockSpec(memory_spac...]
where the time goes in v3:
time: 45.6 us; the launch traced here: 45.4 us
  Pallas kernels  44.7 us (98%)
  between operations  0.66 us (1%)
    pallas_call x1, Pallas kernels, body(): pl.pallas_call(kernel, out_shape=outs, in_specs=[pl.BlockSpec(memory_spac...  42.7 us
    pallas_call x1, Pallas kernels, body(): pl.pallas_call(place_results, out_shape=outs + (row,), in_specs=[pl.Block...  2.02 us

profile of v3, /device:TPU:1, one launch (start us, length us, event | category | flops | bytes accessed | tf_op | source)
XLA Modules:
  0.0 45.4 jit_solution(14841291070375606268)
XLA Ops:
  0.7 42.7 %shard_map.254 = (bf16[128,512]{1,0:T(8,128)(2,1)}, f32[128,512]{1,0:T(8,128)}, f32[1,16]{1,0:T(1,128)}, f32[1,16]{1,0:T(1,128)}, f32[1,16]{1,0:T(1,128)}, /*ind...) custom-call(bf16[128,512]{1,0:T(8,128)(2,1)} %tok_in.1, ...), custom_call_target="tpu_custom_call" | custom-call | tf_op jit(solution)/shard_map/pallas_call | solution.py:586
  43.4 2.0 %shard_map.255 = (bf16[128,512]{1,0:T(8,128)(2,1)}, f32[128,512]{1,0:T(8,128)}, f32[1,16]{1,0:T(1,128)}, f32[1,16]{1,0:T(1,128)}, f32[1,16]{1,0:T(1,128)}, /*ind...) custom-call(bf16[128,512]{1,0:T(8,128)(2,1)} %get-tuple-element.41.r, ...), custom_call_target="tpu_custom_call" | custom-call | tf_op jit(solution)/shard_map/pallas_call | solution.py:597

commit v4 on v3

--- a/solution.py
+++ b/solution.py
@@ -19,7 +19,7 @@
 MESH = pl.DeviceIdType.MESH
 F32 = jnp.float32
 BF16 = jnp.bfloat16
-GRANT = int(62 * 1024 * 1024)
+GRANT = 40 * 1024 * 1024
 
 UP = slice(0, 256)
 QK = slice(256, 384)
@@ -593,14 +593,14 @@
         compiler_params=pltpu.CompilerParams(
             collective_id=0, has_side_effects=True, vmem_limit_bytes=GRANT
         ),
-    )(*operands)
+    )(*(pltpu.with_memory_space_constraint(item, pltpu.HBM) for item in operands))
     results = pl.pallas_call(
         place_results,
         out_shape=outs + (row,),
         in_specs=[pl.BlockSpec(memory_space=pltpu.VMEM)] * 13,
         out_specs=[pl.BlockSpec(memory_space=pl.ANY)] * 14,
         scratch_shapes=[pltpu.SemaphoreType.DMA((14,))],
-        compiler_params=pltpu.CompilerParams(vmem_limit_bytes=GRANT),
+        compiler_params=pltpu.CompilerParams(vmem_limit_bytes=1024 * 1024),
     )(*results)
     (
         output, grad_input, grad_gain1, grad_shift1, grad_gain2, grad_shift2, grad_qkv, grad_qkv_bias, grad_out,

time: 45.6 us -> 43.7 us (0.958)
  Pallas kernels: 44.7 us -> 42.9 us
    pallas_call x1, Pallas kernels: 2.02 us -> 0.97 us  [body(): pl.pallas_call(place_results, out_shape=outs + (row,), in_specs=[pl.Block...]
    pallas_call x1, Pallas kernels: 42.7 us -> 41.9 us  [body(): pl.pallas_call(kernel, out_shape=outs, in_specs=[pl.BlockSpec(memory_spac...]
where the time goes in v4:
time: 43.7 us; the launch traced here: 43.5 us
  Pallas kernels  42.9 us (98%)
  between operations  0.66 us (2%)
    pallas_call x1, Pallas kernels, body(): pl.pallas_call(kernel, out_shape=outs, in_specs=[pl.BlockSpec(memory_spac...  41.9 us
    pallas_call x1, Pallas kernels, body(): pl.pallas_call(place_results, out_shape=outs + (row,), in_specs=[pl.Block...  0.97 us

profile of v4, /device:TPU:1, one launch (start us, length us, event | category | flops | bytes accessed | tf_op | source)
XLA Modules:
  0.0 43.5 jit_solution(14505672768400863869)
XLA Ops:
  0.7 41.9 %shard_map.254 = (bf16[128,512]{1,0:T(8,128)(2,1)S(1)}, f32[128,512]{1,0:T(8,128)S(1)}, f32[1,16]{1,0:T(1,128)S(1)}, f32[1,16]{1,0:T(1,128)S(1)}, f32[1,16]{1,0:...) custom-call(bf16[128,512]{1,0:T(8,128)(2,1)} %tok_in.1, ...), custom_call_target="tpu_custom_call" | custom-call | tf_op jit(solution)/shard_map/pallas_call | solution.py:586
  42.6 1.0 %shard_map.255 = (bf16[128,512]{1,0:T(8,128)(2,1)}, f32[128,512]{1,0:T(8,128)}, f32[1,16]{1,0:T(1,128)}, f32[1,16]{1,0:T(1,128)}, f32[1,16]{1,0:T(1,128)}, /*ind...) custom-call(bf16[128,512]{1,0:T(8,128)(2,1)S(1)} %get-tuple-element., ...), custom_call_target="tpu_custom_call" | custom-call | tf_op jit(solution)/shard_map/pallas_call | solution.py:597

commit v5 on v4

--- a/solution.py
+++ b/solution.py
@@ -380,10 +380,6 @@
     def over_cores(s, own, received, total):
         total[s] = (own[s, c].astype(F32) + received[s].astype(F32)).astype(BF16)
 
-    out_core[0].wait_recv()
-    over_cores(ox, PO, RO, SO)
-    out_across = track(send(M_OUT + 2, SO.at[ox], XO.at[0], dev(ox, c, ot)))
-
     totals = [jnp.zeros((1, 512), F32) for _ in range(4)]
     dx_core = []
     for i, s in enumerate((ox, xh)):
@@ -399,6 +395,10 @@
         term = RSQ[s][:, :1] * (joined - mean_one - n * mean_two)
         PD[s] = term.astype(BF16).reshape(2, 128, 512)
         dx_core.append(track(send(M_DX + i, PD.at[s, oc], RD.at[s], core)))
+        if i == 0:
+            out_core[0].wait_recv()
+            over_cores(ox, PO, RO, SO)
+            out_across = track(send(M_OUT + 2, SO.at[ox], XO.at[0], dev(ox, c, ot)))
 
     up_rows = jnp.concatenate([gb_up[:, :128], gb_up[:, 128:]], axis=0)
     v_row = jnp.concatenate([gb_v, jnp.zeros((1, 128 - HD), F32)], axis=1)
@@ -444,17 +444,11 @@
 
     second_ring(0)
     second_ring(1)
+    second_ring(2)
+    second_ring(3)
     out_across.wait_recv()
     TO[...] = (SO[xh].astype(F32) + XO[0].astype(F32)).astype(BF16)
     out_pair = track(send(M_OUT + 3, TO, XO.at[1], dev(xh, c, ot)))
-
-    second_ring(2)
-    second_ring(3)
-    dx_pair = []
-    for i, part in enumerate(parts_of_rows):
-        dx_across[i].wait_recv()
-        TD[part] = (SD[xh, part].astype(F32) + XD[0, part].astype(F32)).astype(BF16)
-        dx_pair.append(track(send(M_DX + 4 + i, TD.at[part], XD.at[1, part], dev(xh, c, ot))))
 
     for copy in rse1:
         copy.wait_recv()
@@ -476,6 +470,12 @@
     FE[...] = summed(SE[z], RE2).astype(BF16)
     fine = [track(send(M_FINE + i, FE, XF.at[t, xh, c], where)) for i, where in enumerate(group)]
     XF[t, xh, c] = FE[...]
+
+    dx_pair = []
+    for i, part in enumerate(parts_of_rows):
+        dx_across[i].wait_recv()
+        TD[part] = (SD[xh, part].astype(F32) + XD[0, part].astype(F32)).astype(BF16)
+        dx_pair.append(track(send(M_DX + 4 + i, TD.at[part], XD.at[1, part], dev(xh, c, ot))))
 
     for copy in dx_pair:
         copy.wait_recv()

time: 43.7 us -> 41.8 us (0.957)
  Pallas kernels: 42.9 us -> 41 us
    pallas_call x1, Pallas kernels: 41.9 us -> 40 us  [body(): pl.pallas_call(kernel, out_shape=outs, in_specs=[pl.BlockSpec(memory_spac...]
where the time goes in v5:
time: 41.8 us; the launch traced here: 41.6 us
  Pallas kernels  41 us (98%)
  between operations  0.66 us (2%)
    pallas_call x1, Pallas kernels, body(): pl.pallas_call(kernel, out_shape=outs, in_specs=[pl.BlockSpec(memory_spac...  40 us
    pallas_call x1, Pallas kernels, body(): pl.pallas_call(place_results, out_shape=outs + (row,), in_specs=[pl.Block...  0.97 us

profile of v5, /device:TPU:1, one launch (start us, length us, event | category | flops | bytes accessed | tf_op | source)
XLA Modules:
  0.0 41.6 jit_solution(13205014886617666760)
XLA Ops:
  0.7 40.0 %shard_map.254 = (bf16[128,512]{1,0:T(8,128)(2,1)S(1)}, f32[128,512]{1,0:T(8,128)S(1)}, f32[1,16]{1,0:T(1,128)S(1)}, f32[1,16]{1,0:T(1,128)S(1)}, f32[1,16]{1,0:...) custom-call(bf16[128,512]{1,0:T(8,128)(2,1)} %tok_in.1, ...), custom_call_target="tpu_custom_call" | custom-call | tf_op jit(solution)/shard_map/pallas_call | solution.py:586
  40.7 1.0 %shard_map.255 = (bf16[128,512]{1,0:T(8,128)(2,1)}, f32[128,512]{1,0:T(8,128)}, f32[1,16]{1,0:T(1,128)}, f32[1,16]{1,0:T(1,128)}, f32[1,16]{1,0:T(1,128)}, /*ind...) custom-call(bf16[128,512]{1,0:T(8,128)(2,1)S(1)} %get-tuple-element., ...), custom_call_target="tpu_custom_call" | custom-call | tf_op jit(solution)/shard_map/pallas_call | solution.py:597

commit v6 on v5

--- a/solution.py
+++ b/solution.py
@@ -153,6 +153,9 @@
         target[:, DN] = down_cut
         target[:, VO] = vo_cut
 
+    pl.semaphore_wait(barrier, len(peers))
+
+    xw = track(send(M_XW, XS, W.at[z, y, xh], dev(ox, c, t)))
     for load in loads[4:12]:
         load.wait()
     SM[...] = jnp.zeros((16, 128), F32)
@@ -182,11 +185,6 @@
         return jnp.where(row16 < 6, spread, jnp.where(hit, bias, 0.0))
 
     XE[0] = placed(ox).astype(BF16)
-    XE[1] = placed(xh).astype(BF16)
-
-    pl.semaphore_wait(barrier, len(peers))
-
-    xw = track(send(M_XW, XS, W.at[z, y, xh], dev(ox, c, t)))
     xe = track(send(M_XE, XE.at[0], XE.at[2], dev(ox, c, t)))
     across = dev(ox, c, ot)
     core = dev(xh, oc, t)
@@ -198,6 +196,8 @@
     ]
     cot_across = track(send(M_COT, cot_in, CT.at[xh, c], across))
     cot_core = track(send(M_COT + 1, cot_in, CT.at[xh, c], core))
+
+    XE[1] = placed(xh).astype(BF16)
 
     xw.wait_recv()
     ag1 = []
@@ -400,14 +400,6 @@
             over_cores(ox, PO, RO, SO)
             out_across = track(send(M_OUT + 2, SO.at[ox], XO.at[0], dev(ox, c, ot)))
 
-    up_rows = jnp.concatenate([gb_up[:, :128], gb_up[:, 128:]], axis=0)
-    v_row = jnp.concatenate([gb_v, jnp.zeros((1, 128 - HD), F32)], axis=1)
-    for zz in range(4):
-        lanes = slice(zz * 128, (zz + 1) * 128)
-        pieces = [total[:, lanes] for total in totals] + [bias_grad[:, lanes], gb_qk, v_row, up_rows]
-        EG[zz] = jnp.concatenate(pieces + [jnp.zeros((7, 128), F32)], axis=0).astype(BF16)
-    rse1 = [track(send(M_RSE1 + k - 1, EG, RE1.at[k - 1], ydev(k))) for k in (2, 1, 3)]
-
     dx_core[0].wait_recv()
     over_cores(ox, PD, RD, SD)
     parts_of_rows = (slice(0, 64), slice(64, 128))
@@ -419,6 +411,14 @@
     over_cores(xh, PD, RD, SD)
     out_core[1].wait_recv()
     over_cores(xh, PO, RO, SO)
+
+    up_rows = jnp.concatenate([gb_up[:, :128], gb_up[:, 128:]], axis=0)
+    v_row = jnp.concatenate([gb_v, jnp.zeros((1, 128 - HD), F32)], axis=1)
+    for zz in range(4):
+        lanes = slice(zz * 128, (zz + 1) * 128)
+        pieces = [total[:, lanes] for total in totals] + [bias_grad[:, lanes], gb_qk, v_row, up_rows]
+        EG[zz] = jnp.concatenate(pieces + [jnp.zeros((7, 128), F32)], axis=0).astype(BF16)
+    rse1 = [track(send(M_RSE1 + k - 1, EG, RE1.at[k - 1], ydev(k))) for k in (2, 1, 3)]
 
     def summed(own, received):
         total = own.astype(F32)
@@ -477,9 +477,9 @@
         TD[part] = (SD[xh, part].astype(F32) + XD[0, part].astype(F32)).astype(BF16)
         dx_pair.append(track(send(M_DX + 4 + i, TD.at[part], XD.at[1, part], dev(xh, c, ot))))
 
-    for copy in dx_pair:
-        copy.wait_recv()
-    gin_o[...] = CT[xh, c].astype(F32) + (TD[...].astype(F32) + XD[1].astype(F32))
+    early = len(sent) - len(fin) - len(fine) - len(dx_pair)
+    for copy in sent[:early]:
+        copy.wait_send()
 
     out_pair.wait_recv()
     total = TO[...].astype(F32) + XO[1].astype(F32)
@@ -505,6 +505,10 @@
             wide = slice((xx * 2 + cc) * 256, (xx * 2 + cc + 1) * 256)
             gupw_o[:, wide] = both[cc][:, UP]
             gdownw_o[:, wide] = both[cc][:, DN]
+
+    for copy in dx_pair:
+        copy.wait_recv()
+    gin_o[...] = CT[xh, c].astype(F32) + (TD[...].astype(F32) + XD[1].astype(F32))
 
     for copy in fine:
         copy.wait_recv()
@@ -537,7 +541,7 @@
     for which in range(3):
         gqkvb_o[which] = new_qkv[which]
     gupb_o[...] = new_up
-    for copy in sent:
+    for copy in sent[early:]:
         copy.wait_send()
 
 

time: 41.8 us -> 41.6 us (level)
  no operation moved by 1% of the time
where the time goes in v6:
time: 41.6 us; the launch traced here: 41.5 us
  Pallas kernels  40.9 us (98%)
  between operations  0.66 us (2%)
    pallas_call x1, Pallas kernels, body(): pl.pallas_call(kernel, out_shape=outs, in_specs=[pl.BlockSpec(memory_spac...  39.9 us
    pallas_call x1, Pallas kernels, body(): pl.pallas_call(place_results, out_shape=outs + (row,), in_specs=[pl.Block...  0.97 us

profile of v6, /device:TPU:1, one launch (start us, length us, event | category | flops | bytes accessed | tf_op | source)
XLA Modules:
  0.0 41.5 jit_solution(14334897013198288997)
XLA Ops:
  0.7 39.9 %shard_map.254 = (bf16[128,512]{1,0:T(8,128)(2,1)S(1)}, f32[128,512]{1,0:T(8,128)S(1)}, f32[1,16]{1,0:T(1,128)S(1)}, f32[1,16]{1,0:T(1,128)S(1)}, f32[1,16]{1,0:...) custom-call(bf16[128,512]{1,0:T(8,128)(2,1)} %tok_in.1, ...), custom_call_target="tpu_custom_call" | custom-call | tf_op jit(solution)/shard_map/pallas_call | solution.py:590
  40.5 1.0 %shard_map.255 = (bf16[128,512]{1,0:T(8,128)(2,1)}, f32[128,512]{1,0:T(8,128)}, f32[1,16]{1,0:T(1,128)}, f32[1,16]{1,0:T(1,128)}, f32[1,16]{1,0:T(1,128)}, /*ind...) custom-call(bf16[128,512]{1,0:T(8,128)(2,1)S(1)} %get-tuple-element., ...), custom_call_target="tpu_custom_call" | custom-call | tf_op jit(solution)/shard_map/pallas_call | solution.py:601
